TPU v7x, 32 devices: a whole 2x2x4 slice. The times are simulated.
32 devices in a mesh: ctx: 4 (over z), exp: 8 (over y, x, core).
Axes of the slice: x: 2, y: 2, z: 4, core: 2. Of those that a mesh axis runs over, the one named last changes fastest.
Arguments:
- q_nope: bfloat16 [1024, 16384], P('ctx', 'exp'), may hold values from -6 to 6
- q_rope: bfloat16 [1024, 8192], P('ctx', 'exp'), may hold values from -24 to 24
- kv_latent: bfloat16 [1024, 512], P('ctx'), may hold values from -6 to 6
- key_rope: bfloat16 [1024, 64], P('ctx'), may hold values from -6 to 6
- w_uk: bfloat16 [128, 128, 512], P('exp'), may hold values from -0.5 to 0.5
- w_uv: bfloat16 [128, 512, 128], P('exp'), may hold values from -1 to 1
- w_out: bfloat16 [16384, 7168], P('exp', 'ctx'), may hold values from -0.09375 to 0.09375
- w_gate: bfloat16 [8, 7168, 2048], P('exp', 'ctx'), may hold values from -0.0625 to 0.0625
- w_up: bfloat16 [8, 7168, 2048], P('exp', 'ctx'), may hold values from -0.0625 to 0.0625
- w_down: bfloat16 [8, 2048, 7168], P('exp', None, 'ctx'), may hold values from -0.125 to 0.125
- route_ids: int32 [1024, 4], P('exp'), may hold values from 0 to 7, all different within a row; in each aligned block of 128 rows (0 to 127, 128 to 255, ...) at most 96 rows name the same one
- route_gates: bfloat16 [1024, 4], P('exp'), may hold values from 0.19921875 to 1
Outputs:
- attn_out: bfloat16 [1024, 7168], P('exp', 'ctx')
- moe_out: bfloat16 [1024, 7168], P('exp', 'ctx')
Inputs may be any that keep to these rules, and one draw needn't show every extreme that they name: `route_ids`: each row names 4 different experts. In each aligned block of 128 rows no expert is named by more than 96 rows, and in some block one expert is named by exactly 96 rows.
All inputs are finite; a program needn't handle non-finite values.
Results may differ from a plain program's by a relative error of at most 0.035.
Values may be sent and summed in bfloat16 or wider, within the bound.
A program may use at most 128 MiB of HBM per device.

v0:
```python
from functools import partial
import math

import jax
import jax.numpy as jnp
from jax import lax
from jax.sharding import PartitionSpec as P

NEG_FILL = -1e30


def score_block(running, pieces, key_start, query_latent, query_rope, query_pos, score_scale):
    running_max, running_sum, running_acc = running
    latent_piece, rope_piece = pieces
    scores = jnp.einsum(
        "ihc,jc->ihj", query_latent, latent_piece, preferred_element_type=jnp.float32
    )
    scores = scores + jnp.einsum(
        "ihr,jr->ihj", query_rope, rope_piece, preferred_element_type=jnp.float32
    )
    scores = scores * score_scale
    key_pos = jnp.arange(latent_piece.shape[0], dtype=jnp.int32)
    allowed = (key_pos[None, :] <= query_pos[:, None])[:, None, :]
    block_max = jnp.max(jnp.where(allowed, scores, NEG_FILL), axis=2)
    new_max = jnp.maximum(running_max, block_max)
    exp_terms = jnp.where(allowed, jnp.exp(scores - new_max[:, :, None]), 0.0)
    new_sum = jnp.sum(exp_terms, axis=2)
    update = jnp.einsum(
        "ihj,jc->ihc",
        exp_terms.astype(jnp.bfloat16),
        latent_piece,
        preferred_element_type=jnp.float32,
    )
    return (new_max, new_sum, update)


def local(
    q_nope,
    q_rope,
    kv_latent,
    key_rope,
    w_uk,
    w_uv,
    w_out,
    w_gate,
    w_up,
    w_down,
    route_ids,
    route_gates,
):
    tok_rows = q_nope.shape[0]
    head_count, nope_size, latent_size = w_uk.shape
    rope_size = key_rope.shape[1]
    score_scale = 1.0 / math.sqrt(nope_size + rope_size)
    ctx_here = lax.axis_index("ctx")
    query_pos = ctx_here * tok_rows + jnp.arange(tok_rows, dtype=jnp.int32)
    query_latent = jnp.einsum(
        "ihd,hdc->ihc",
        q_nope.reshape(tok_rows, head_count, nope_size),
        w_uk,
        preferred_element_type=jnp.float32,
    ).astype(jnp.bfloat16)
    query_rope = q_rope.reshape(tok_rows, head_count, rope_size)
    initial = (
        jnp.full((tok_rows, head_count), NEG_FILL, jnp.float32),
        jnp.zeros((tok_rows, head_count), jnp.float32),
        jnp.zeros((tok_rows, head_count, latent_size), jnp.float32),
    )
    step_fn = partial(
        score_block,
        query_latent=query_latent,
        query_rope=query_rope,
        query_pos=query_pos,
        score_scale=score_scale,
    )
    attended = step_fn(
        initial,
        (
            lax.all_gather(kv_latent, "ctx", axis=0, tiled=True),
            lax.all_gather(key_rope, "ctx", axis=0, tiled=True),
        ),
        jnp.int32(0),
    )
    latent_out = (attended[2] / attended[1][:, :, None]).astype(jnp.bfloat16)
    head_out = jnp.einsum(
        "ihc,hcv->ihv", latent_out, w_uv, preferred_element_type=jnp.float32
    ).astype(jnp.bfloat16)
    gathered = lax.all_gather(head_out.reshape(tok_rows, -1), "ctx", axis=0, tiled=True)
    out_rows = gathered.shape[0] // lax.axis_size("exp")
    attn_out = lax.psum_scatter(
        jnp.dot(gathered, w_out, preferred_element_type=jnp.float32).astype(jnp.bfloat16),
        "exp",
        scatter_dimension=0,
        tiled=True,
    )
    feature_cols = attn_out.shape[1]
    top_count = route_ids.shape[1]
    expert_count = lax.axis_size("exp") * w_gate.shape[0]
    capacity = 3 * out_rows * top_count // (2 * expert_count)
    slot_total = expert_count * capacity
    flat_ids = route_ids.reshape(-1)
    onehot = (flat_ids[:, None] == jnp.arange(expert_count, dtype=jnp.int32)[None, :]).astype(
        jnp.int32
    )
    earlier = jnp.cumsum(onehot, axis=0) - onehot
    slot_ids = jnp.sum(earlier * onehot, axis=1)
    targets = (flat_ids * capacity + slot_ids).reshape(out_rows, top_count)
    slot_range = jnp.arange(slot_total, dtype=jnp.int32)
    hits = targets[:, :, None] == slot_range[None, None, :]
    placing = jnp.sum(hits.astype(jnp.float32), axis=1).astype(jnp.bfloat16).T
    send_rows = jnp.dot(placing, attn_out, preferred_element_type=jnp.float32).astype(jnp.bfloat16)
    send_rows = send_rows.reshape(expert_count, capacity, feature_cols)
    weighting = jnp.sum(
        jnp.where(hits, route_gates[:, :, None], jnp.zeros((), jnp.bfloat16)), axis=1
    )
    arrived = lax.all_to_all(send_rows, "exp", split_axis=0, concat_axis=0, tiled=True)
    source_count = arrived.shape[0]
    item_count = arrived.shape[1]
    flat_rows = arrived.reshape(source_count * item_count, feature_cols)
    gate_part = jnp.dot(flat_rows, w_gate[0], preferred_element_type=jnp.float32)
    up_part = jnp.dot(flat_rows, w_up[0], preferred_element_type=jnp.float32)
    gate_pre = lax.psum(gate_part.astype(jnp.bfloat16), "ctx").astype(jnp.float32)
    up_pre = lax.psum(up_part.astype(jnp.bfloat16), "ctx").astype(jnp.float32)
    hidden = (jax.nn.silu(gate_pre) * up_pre).astype(jnp.bfloat16)
    expert_out = jnp.dot(hidden, w_down[0], preferred_element_type=jnp.float32).astype(jnp.bfloat16)
    expert_out = expert_out.reshape(source_count, item_count, feature_cols)
    returned = lax.all_to_all(expert_out, "exp", split_axis=0, concat_axis=0, tiled=True)
    moe_out = jnp.dot(
        weighting, returned.reshape(slot_total, feature_cols), preferred_element_type=jnp.float32
    ).astype(jnp.bfloat16)
    return (attn_out, moe_out)


def solution(mesh):
    placed = (
        P("ctx", "exp"),
        P("ctx", "exp"),
        P("ctx", None),
        P("ctx", None),
        P("exp", None, None),
        P("exp", None, None),
        P("exp", "ctx"),
        P("exp", "ctx", None),
        P("exp", "ctx", None),
        P("exp", None, "ctx"),
        P("exp", None),
        P("exp", None),
    )
    return jax.shard_map(
        local,
        mesh=mesh,
        in_specs=placed,
        out_specs=(P("exp", "ctx"), P("exp", "ctx")),
        check_vma=False,
    )
```

profile of v0, /device:TPU:0, one launch (start us, length us, event | category | flops | bytes accessed | tf_op | source)
XLA Modules:
  0.0 560.5 jit_solution(6260192014938379999)
XLA Ops:
  7.2 0.7 all-gather.3.cloned.1.call-update
  8.0 2.1 copy.38
  10.0 15.3 %all_gather.10 = bf16[1024,64]{0,1:T(8,128)(2,1)S(1)} all-gather(bf16[256,64]{0,1:T(8,128)(2,1)} %param.15), channel_id=1, replica_groups=mesh['ctx'=4,'exp'=8] {'ctx'}, dimensions={0}, use_global_device_ids=true | all-gather | bytes 163840 | tf_op jit(solution)/shard_map/all_gather | solution.py:80
  25.4 0.2 iota_compare_fusion.1
  25.6 15.0 %all-gather.3.cloned.1.call-done = bf16[1024,512]{1,0:T(8,128)(2,1)} async-done(((bf16[256,512]{1,0:T(8,128)(2,1)}), bf16[1024,512]{1,0:T(8,128)(2,1)}) %all-gather.3.cloned.1.call-update) | async-done | bytes 1048592 | tf_op jit(solution)/shard_map/all_gather | solution.py:79
  40.6 10.5 %fusion.18 = f32[256,16,1024]{2,0,1:T(8,128)} fusion(bf16[16,128,512]{2,1,0:T(8,128)(2,1)S(1)} %copy-done, bf16[1024,512]{1,0:T(8,128)(2,1)} %all-gather.3.cloned.1.call-done, bf16[256,2048]{1,0:T(8,128)(2,1)} %param.12), kind=kOutput, calls=%fused_computation.23 | convolution fusion | flops 4833935360 | bytes 20971520 | tf_op jit(solution)/shard_map/ihc,jc->ihj/dot_general | solution.py:15
  51.1 8.1 %select_reduce_fusion = (f32[256,16]{0,1:T(8,128)S(1)}, f32[256,16,1024]{2,0,1:T(8,128)S(1)}) fusion(pred[256,1024]{1,0:T(8,128)(4,1)S(1)} %iota_compare_fusion.1, f32[256,16,1024]{2,0,1:T(8,128)} %fusion.18, bf16[256,16,64]{0,2,1:T(8,128)(2,1)} %bitcast.69, bf16[1024,64]{0,1:T(8,128)(2,1)S(1)} %all_gather.10), kind=kOutput, calls=%fused_computation.1 | convolution fusion | flops 553644032 | bytes 34488320 | tf_op jit(solution)/shard_map/ihr,jr->ihj/dot_general | solution.py:18
  59.3 5.7 %copy-done.2 = f32[256,16,1024]{2,0,1:T(8,128)} copy-done((f32[256,16,1024]{2,0,1:T(8,128)}, f32[256,16,1024]{2,0,1:T(8,128)S(1)}, u32[]{:S(2)}) %copy-start.2) | copy-done | bytes 16777240
  65.0 4.3 fusion
  69.3 11.9 %fusion.40 = bf16[16,256,128]{1,2,0:T(8,128)(2,1)} fusion(bf16[16,512,128]{2,1,0:T(8,128)(2,1)} %param.17, f32[256,16]{0,1:T(8,128)S(1)} %fusion, f32[256,16,1024]{2,0,1:T(8,128)} %copy-done.2, f32[256,16]{0,1:T(8,128)S(1)} %broadcast_maximum_fusion, pred[256,1024]{1,0:T(8,128)(4,1)S(1)} %iota_compare_fusion.1, bf16[1024,512]{1,0:T(8,128)(2,1)S(1)} %copy-done.5), kind=kOutput, calls=%fused_computation.38 | convolution fusion | flops 4849139712 | bytes 21266432 | tf_op jit(solution)/shard_map/ihc,hcv->ihv/dot_general | solution.py:85
  81.2 0.2 reduce-scatter.2.cloned.1.call-start
  81.4 80.1 %all-gather.5.cloned.1.call-done = bf16[1024,2048]{0,1:T(8,128)(2,1)} async-done(((bf16[256,2048]{0,1:T(8,128)(2,1)}), bf16[1024,2048]{0,1:T(8,128)(2,1)}) %all-gather.5.cloned.1.call-update) | async-done | bytes 4194320 | tf_op jit(solution)/shard_map/all_gather | solution.py:88
  161.6 13.1 %convolution_convert_fusion = bf16[1024,1792]{1,0:T(8,128)(2,1)} fusion(bf16[1024,2048]{0,1:T(8,128)(2,1)} %all-gather.5.cloned.1.call-done, bf16[2048,1792]{1,0:T(8,128)(2,1)} %param.18), kind=kOutput, calls=%fused_computation.27 | convolution fusion | flops 7518027776 | bytes 15204352 | tf_op jit(solution)/shard_map/dot_general | solution.py:91
  174.8 0.1 copy.40
  174.9 0.1 eq.42
  175.0 0.1 eq.38
  175.1 1.1 reduce-window.6
  176.3 0.2 slice_reduce_fusion
  176.5 0.1 fusion.54
  176.6 0.1 reduce_sum.43
  176.8 0.3 convert_reduce_fusion
  177.1 44.7 %reduce-scatter.2.cloned.1.call-done = bf16[128,1792]{1,0:T(8,128)(2,1)} async-done(((bf16[1024,1792]{1,0:T(8,128)(2,1)}), bf16[128,1792]{1,0:T(8,128)(2,1)}) %reduce-scatter.2.cloned.1.call-update) | async-done | bytes 458768 | tf_op jit(solution)/shard_map/reduce_scatter | solution.py:90
  221.8 1.9 convolution_convert_fusion.1
  223.7 36.4 %all_to_all.10 = bf16[8,96,1792]{2,1,0:T(8,128)(2,1)S(1)} all-to-all(bf16[8,96,1792]{2,1,0:T(8,128)(2,1)S(1)} %bitcast.65), channel_id=1, replica_groups=mesh['ctx'=4,'exp'=8] {'exp'}, dimensions={0} | all-to-all | bytes 5505024 | tf_op jit(solution)/shard_map/all_to_all | solution.py:116
  260.2 10.4 %fusion.22 = bf16[768,2048]{1,0:T(8,128)(2,1)} fusion(bf16[768,1792]{1,0:T(8,128)(2,1)S(1)} %bitcast.67, bf16[1,1792,2048]{2,1,0:T(8,128)(2,1)} %param.19), kind=kOutput, calls=%fused_computation.29 | convolution fusion | flops 5638717440 | bytes 13238272 | tf_op jit(solution)/shard_map/dot_general | solution.py:120
  270.6 7.3 %fusion.25 = bf16[768,2048]{1,0:T(8,128)(2,1)} fusion(bf16[768,1792]{1,0:T(8,128)(2,1)S(1)} %bitcast.68, bf16[1,1792,2048]{2,1,0:T(8,128)(2,1)S(1)} %bitcast.72), kind=kOutput, calls=%fused_computation.30 | convolution fusion | flops 5638717440 | bytes 13238272 | tf_op jit(solution)/shard_map/dot_general | solution.py:121
  277.9 222.5 %all-reduce.3.cloned.1.call-done = (bf16[768,2048]{1,0:T(8,128)(2,1)}, bf16[768,2048]{1,0:T(8,128)(2,1)}) async-done(((bf16[768,2048]{1,0:T(8,128)(2,1)}, bf16[768,2048]{1,0:T(8,128)(2,1)}), (bf16[768,2048]{1,0:T(8,128)(2,1)}, bf16[768,2048]{1,0:T(8,128)(2,1)})) %all-reduce.3.cloned.1.call-update) | async-done | bytes 6291472 | tf_op jit(solution)/shard_map/psum | solution.py:123
  500.3 12.5 %fusion.28 = bf16[768,1792]{1,0:T(8,128)(2,1)} fusion(bf16[1,2048,1792]{2,1,0:T(8,128)(2,1)} %param.21, bf16[768,2048]{1,0:T(8,128)(2,1)} %get-tuple-element.2, bf16[768,2048]{1,0:T(8,128)(2,1)} %get-tuple-element.3), kind=kOutput, calls=%fused_computation.31 | convolution fusion | flops 5651103744 | bytes 16384000 | tf_op jit(solution)/shard_map/dot_general | solution.py:125
  512.8 4.4 all-to-all-start.1
  517.2 0.2 fusion.50
  517.5 33.4 %all-to-all-done.1 = bf16[8,96,1792]{2,1,0:T(8,128)(2,1)} async-done(((bf16[8,96,1792]{2,1,0:T(8,128)(2,1)}), bf16[8,96,1792]{2,1,0:T(8,128)(2,1)}, u32[]{:S(2)}, u32[]{:S(2)}) %all-to-all-start.1) | async-done | bytes 2752544 | tf_op jit(solution)/shard_map/all_to_all | solution.py:127
  550.9 3.1 convolution_convert_fusion.2
  (29 shorter events, 0.3 us)
Async XLA Ops:
  7.2 33.4 %copy-start = (bf16[16,128,512]{2,1,0:T(8,128)(2,1)S(1)}, bf16[16,128,512]{2,1,0:T(8,128)(2,1)}, u32[]{:S(2)}) copy-start(bf16[16,128,512]{2,1,0:T(8,128)(2,1)} %param.16) | copy-start | bytes 6291460
  7.2 33.4 %all-gather.3.cloned.1.call-start = ((), (), s32[]{:S(2)}) async-start(), calls=%async_computation.3 | async-start | bytes 1310720 | tf_op jit(solution)/shard_map/all_gather | solution.py:79
  7.9 153.7 %all-gather.5.cloned.1.call-start = ((), (), s32[]{:S(2)}) async-start(), calls=%async_computation.4 | async-start | bytes 5242880 | tf_op jit(solution)/shard_map/all_gather | solution.py:88
  59.2 5.7 %copy-start.2 = (f32[256,16,1024]{2,0,1:T(8,128)}, f32[256,16,1024]{2,0,1:T(8,128)S(1)}, u32[]{:S(2)}) copy-start(f32[256,16,1024]{2,0,1:T(8,128)S(1)} %get-tuple-element.5) | copy-start | bytes 50331652
  65.0 4.3 copy-start.5
  81.2 93.6 %copy-start.3 = (s32[128,4]{0,1:T(4,128)S(1)}, s32[128,4]{0,1:T(4,128)}, u32[]{:S(2)}) copy-start(s32[128,4]{0,1:T(4,128)} %param.22) | copy-start | bytes 6148
  81.2 140.6 %reduce-scatter.2.cloned.1.call-start = ((), (), s32[]{:S(2)}) async-start(), calls=%async_computation.5 | async-start | bytes 4128768 | tf_op jit(solution)/shard_map/reduce_scatter | solution.py:90
  174.7 325.6 %all-reduce.3.cloned.1.call-start = ((), (), s32[]{:S(2)}) async-start(), calls=%async_computation.6 | async-start | bytes 12582912 | tf_op jit(solution)/shard_map/psum | solution.py:123
  223.7 46.8 %slice-start = ((s8[7340032]{0:T(1024)(128)(4,1)}), s8[4194304]{0:T(1024)(128)(4,1)S(1)}, s32[]{:S(2)}) async-start(s8[7340032]{0:T(1024)(128)(4,1)} %bitcast.71), calls=%async_computation.7 | async-start | bytes 8388608
  260.2 10.4 %slice-start.1 = ((s8[7340032]{0:T(1024)(128)(4,1)}), s8[3145728]{0:T(1024)(128)(4,1)S(1)}, s32[]{:S(2)}) async-start(s8[7340032]{0:T(1024)(128)(4,1)} %bitcast.71), calls=%async_computation.8 | async-start | bytes 6291456
  500.3 16.9 %copy-start.4 = (bf16[128,4]{0,1:T(4,128)(2,1)S(1)}, bf16[128,4]{0,1:T(4,128)(2,1)}, u32[]{:S(2)}) copy-start(bf16[128,4]{0,1:T(4,128)(2,1)} %param.23) | copy-start | bytes 3076
  500.3 53.7 %copy-start.1 = (bf16[16,128,512]{2,1,0:T(8,128)(2,1)S(1)}, bf16[16,128,512]{2,1,0:T(8,128)(2,1)}, u32[]{:S(2)}) copy-start(bf16[16,128,512]{2,1,0:T(8,128)(2,1)} %param.16) | copy-start | bytes 6291460
  512.8 38.1 %all-to-all-start.1 = ((bf16[8,96,1792]{2,1,0:T(8,128)(2,1)}), bf16[8,96,1792]{2,1,0:T(8,128)(2,1)}, u32[]{:S(2)}, u32[]{:S(2)}) async-start(bf16[8,96,1792]{2,1,0:T(8,128)(2,1)} %bitcast.66), calls=%async_computation.2 | async-start | bytes 5505024 | tf_op jit(solution)/shard_map/all_to_all | solution.py:127
Sparse Core Ops, SparseCore 0:
  9.6 30.9 all-gather.2
  81.3 80.2 all-gather.4
  174.9 46.9 reduce-scatter.1
  278.0 222.2 all-reduce.2
where the time goes:
time: 561 us
  waiting for transfers between devices  396 us (71%)
  matrix products  78.8 us (14%)
  blocking collectives  51.8 us (9%)
  between operations  13.9 us (2%)
  local copies, waits for them, and re-layouts  8.52 us (2%)
  other arithmetic  6.31 us (1%)
    psum x1, waiting for transfers between devices, local(): up_pre = lax.psum(up_part.astype(jnp.bfloat16), 'ctx').astype(jnp.float32)  222 us
    all_gather x1, waiting for transfers between devices, local(): lax.all_gather(head_out.reshape(tok_rows, -1), 'ctx', axis=0, tiled=True)  80.1 us
    reduce_scatter x1, waiting for transfers between devices, local(): lax.psum_scatter(jnp.dot(gathered, w_out, preferred_element_type=jnp.floa...  44.7 us
    all_to_all x1, blocking collectives, local(): lax.all_to_all(send_rows, 'exp', split_axis=0, concat_axis=0, tiled=True)  36.4 us
    all_to_all x1, waiting for transfers between devices, local(): lax.all_to_all(expert_out, 'exp', split_axis=0, concat_axis=0, tiled=True)  33.4 us
    all_gather x1, blocking collectives, local(): lax.all_gather(key_rope, 'ctx', axis=0, tiled=True)  15.3 us
    all_gather x1, waiting for transfers between devices, local(): lax.all_gather(kv_latent, 'ctx', axis=0, tiled=True)  15 us
    dot_general x1, matrix products, local(): jnp.dot(gathered, w_out, preferred_element_type=jnp.float32)  13.1 us
  transfers between devices with their start and end apart: 5, of which 5 were waited for; matrix products, arithmetic and copies ran while one was open for 1% of the time, Pallas kernels for 0%

commit v1 on v0

--- a/solution.py
+++ b/solution.py
@@ -4,9 +4,220 @@
 import jax
 import jax.numpy as jnp
 from jax import lax
+from jax.experimental import pallas as pl
+from jax.experimental.pallas import tpu as pltpu
 from jax.sharding import PartitionSpec as P
 
 NEG_FILL = -1e30
+MESH = pl.DeviceIdType.MESH
+CHUNK = 16
+BLOCK = 128
+
+
+def expert_kernel(
+    n_ctx, x, wg_hbm, wu_hbm, wd_hbm, out, wg, wu, wd, part, held, hid,
+    w_sem, rs_send, rs_recv, ag_send, ag_recv,
+):
+    p = lax.axis_index("ctx")
+    last = n_ctx - 1
+    rows = x.shape[0]
+    half = rows // 2
+    ff = wg.shape[1]
+    n = half // CHUNK
+    per = BLOCK // CHUNK
+    blocks = half // BLOCK
+    tile = 512 if ff % 512 == 0 else ff
+
+    loads = [
+        pltpu.make_async_copy(src, dst, w_sem.at[i])
+        for i, (src, dst) in enumerate(((wg_hbm, wg), (wu_hbm, wu), (wd_hbm, wd)))
+    ]
+    for load in loads:
+        load.start()
+
+    barrier = pltpu.get_barrier_semaphore()
+
+    @pl.when(p > 0)
+    def _():
+        pl.semaphore_signal(barrier, inc=1, device_id={"ctx": p - 1}, device_id_type=MESH)
+
+    @pl.when(p < last)
+    def _():
+        pl.semaphore_signal(barrier, inc=1, device_id={"ctx": p + 1}, device_id_type=MESH)
+
+    pl.semaphore_wait(barrier, (p > 0).astype(jnp.int32) + (p < last).astype(jnp.int32))
+
+    ahead = (jnp.minimum(p + 1, last), jnp.maximum(p - 1, 0))
+
+    def chunk_rows(d, t):
+        return pl.ds(pl.multiple_of(d * half + t * CHUNK, CHUNK), CHUNK)
+
+    def rs_copy(d, t, src):
+        at = chunk_rows(d, t)
+        return pltpu.make_async_remote_copy(
+            src_ref=src.at[at],
+            dst_ref=held.at[at],
+            send_sem=rs_send.at[d * n + t],
+            recv_sem=rs_recv.at[d * n + t],
+            device_id={"ctx": ahead[d]},
+            device_id_type=MESH,
+        )
+
+    def ag_copy(d, t):
+        at = chunk_rows(d, t)
+        return pltpu.make_async_remote_copy(
+            src_ref=hid.at[at],
+            dst_ref=hid.at[at],
+            send_sem=ag_send.at[d * n + t],
+            recv_sem=ag_recv.at[d * n + t],
+            device_id={"ctx": ahead[1 - d]},
+            device_id_type=MESH,
+        )
+
+    def gate_up(d, block):
+        at = pl.ds(pl.multiple_of(d * half + block * BLOCK, BLOCK), BLOCK)
+
+        @pl.loop(0, ff // tile)
+        def _(c):
+            base = pl.multiple_of(c * tile, tile)
+            above = pl.multiple_of(ff + c * tile, tile)
+            part[at, pl.ds(base, tile)] = jnp.dot(
+                x[at, :], wg[:, pl.ds(base, tile)], preferred_element_type=jnp.float32
+            ).astype(part.dtype)
+            part[at, pl.ds(above, tile)] = jnp.dot(
+                x[at, :], wu[:, pl.ds(base, tile)], preferred_element_type=jnp.float32
+            ).astype(part.dtype)
+
+    width = out.shape[1]
+    down_tile = 256 if width % 256 == 0 else 128
+
+    def down(d, block):
+        at = pl.ds(pl.multiple_of(d * half + block * BLOCK, BLOCK), BLOCK)
+
+        @pl.loop(0, width // down_tile)
+        def _(c):
+            cols = pl.ds(pl.multiple_of(c * down_tile, down_tile), down_tile)
+            out[at, cols] = jnp.dot(
+                hid[at, :], wd[:, cols], preferred_element_type=jnp.float32
+            ).astype(out.dtype)
+
+    first = (2 * p > last).astype(jnp.int32)
+    loads[0].wait()
+    loads[1].wait()
+    gate_up(first, 0)
+
+    @pl.loop(0, n + 2 * last)
+    def _(s):
+        for d in range(2):
+            k = p if d == 0 else last - p
+            t = s - k
+
+            @pl.when((t >= 0) & (t < n))
+            def _():
+                at = chunk_rows(d, t)
+
+                @pl.when(k == 0)
+                def _():
+                    rs_copy(d, t, part).start()
+
+                @pl.when((k > 0) & (k < last))
+                def _():
+                    rs_copy(d, t, held).wait_recv()
+                    held[at, :] = (
+                        held[at, :].astype(jnp.float32) + part[at, :].astype(jnp.float32)
+                    ).astype(held.dtype)
+                    rs_copy(d, t, held).start()
+
+                @pl.when(k == last)
+                def _():
+                    rs_copy(d, t, held).wait_recv()
+                    gate = held[at, pl.ds(0, ff)].astype(jnp.float32) + part[
+                        at, pl.ds(0, ff)
+                    ].astype(jnp.float32)
+                    up = held[at, pl.ds(ff, ff)].astype(jnp.float32) + part[
+                        at, pl.ds(ff, ff)
+                    ].astype(jnp.float32)
+                    hid[at, :] = (gate / (1.0 + jnp.exp(-gate)) * up).astype(hid.dtype)
+                    ag_copy(d, t).start()
+
+        for d in range(2):
+            j = last - p if d == 0 else p
+            u = s - last - j
+
+            @pl.when((u >= 0) & (u < n))
+            def _():
+                @pl.when(j > 0)
+                def _():
+                    ag_copy(d, u).wait_recv()
+
+                    @pl.when(j < last)
+                    def _():
+                        ag_copy(d, u).start()
+
+        i = s + 1
+
+        @pl.when(i < 2 * blocks)
+        def _():
+            gate_up((i + first) % 2, i // 2)
+
+        @pl.when(s == last)
+        def _():
+            loads[2].wait()
+
+        for d in range(2):
+            j = last - p if d == 0 else p
+            u = s - last - j
+
+            @pl.when((u >= 0) & (u < n) & (u % per == per - 1))
+            def _():
+                down(d, u // per)
+
+    @pl.loop(0, n)
+    def _(t):
+        for d in range(2):
+            k = p if d == 0 else last - p
+
+            @pl.when(k < last)
+            def _():
+                rs_copy(d, t, held).wait_send()
+
+            @pl.when(k > 0)
+            def _():
+                ag_copy(d, t).wait_send()
+
+
+def expert_layer(rows_in, gate_w, up_w, down_w):
+    n_ctx = lax.axis_size("ctx")
+    rows, width = rows_in.shape
+    ff = gate_w.shape[1]
+    n = rows // 2 // CHUNK
+    return pl.pallas_call(
+        partial(expert_kernel, n_ctx),
+        out_shape=jax.ShapeDtypeStruct((rows, width), jnp.bfloat16),
+        in_specs=[pl.BlockSpec(memory_space=pltpu.VMEM)]
+        + [pl.BlockSpec(memory_space=pl.ANY)] * 3,
+        out_specs=pl.BlockSpec(memory_space=pltpu.VMEM),
+        scratch_shapes=[
+            pltpu.VMEM((width, ff), jnp.bfloat16),
+            pltpu.VMEM((width, ff), jnp.bfloat16),
+            pltpu.VMEM((ff, width), jnp.bfloat16),
+            pltpu.VMEM((rows, 2 * ff), jnp.bfloat16),
+            pltpu.VMEM((rows, 2 * ff), jnp.bfloat16),
+            pltpu.VMEM((rows, ff), jnp.bfloat16),
+            pltpu.SemaphoreType.DMA((3,)),
+            pltpu.SemaphoreType.DMA((2 * n,)),
+            pltpu.SemaphoreType.DMA((2 * n,)),
+            pltpu.SemaphoreType.DMA((2 * n,)),
+            pltpu.SemaphoreType.DMA((2 * n,)),
+        ],
+        compiler_params=pltpu.CompilerParams(
+            collective_id=0, has_side_effects=True, vmem_limit_bytes=56 * 1024 * 1024
+        ),
+        cost_estimate=pl.CostEstimate(
+            flops=6 * rows * width * ff, bytes_accessed=6 * width * ff, transcendentals=rows * ff
+        ),
+        name="expert_layer",
+    )(rows_in, gate_w, up_w, down_w)
 
 
 def score_block(running, pieces, key_start, query_latent, query_rope, query_pos, score_scale):
@@ -117,12 +328,7 @@
     source_count = arrived.shape[0]
     item_count = arrived.shape[1]
     flat_rows = arrived.reshape(source_count * item_count, feature_cols)
-    gate_part = jnp.dot(flat_rows, w_gate[0], preferred_element_type=jnp.float32)
-    up_part = jnp.dot(flat_rows, w_up[0], preferred_element_type=jnp.float32)
-    gate_pre = lax.psum(gate_part.astype(jnp.bfloat16), "ctx").astype(jnp.float32)
-    up_pre = lax.psum(up_part.astype(jnp.bfloat16), "ctx").astype(jnp.float32)
-    hidden = (jax.nn.silu(gate_pre) * up_pre).astype(jnp.bfloat16)
-    expert_out = jnp.dot(hidden, w_down[0], preferred_element_type=jnp.float32).astype(jnp.bfloat16)
+    expert_out = expert_layer(flat_rows, w_gate[0], w_up[0], w_down[0])
     expert_out = expert_out.reshape(source_count, item_count, feature_cols)
     returned = lax.all_to_all(expert_out, "exp", split_axis=0, concat_axis=0, tiled=True)
     moe_out = jnp.dot(

time: 561 us -> 455 us (0.81)
  waiting for transfers between devices: 396 us -> 174 us
  Pallas kernels: 0 us -> 147 us
  matrix products: 78.8 us -> 48.7 us
    psum x1 -> x0, waiting for transfers between devices: 222 us -> none  [local(): up_pre = lax.psum(up_part.astype(jnp.bfloat16), 'ctx').astype(jnp.float32)]
    pallas_call x0 -> x1, Pallas kernels: none -> 147 us  [expert_layer(): pl.pallas_call(partial(expert_kernel, n_ctx), out_shape=jax.ShapeDtypeStr...]
    dot_general x3 -> x0, matrix products: 30.2 us -> none  [the longest x1 12.5 us: local(): jnp.dot(hidden, w_down[0], preferred_element_type=jnp.float32)]
  transfers between devices with their start and end apart: 5 -> 4, of which waited for: 5 -> 4; matrix products, arithmetic and copies ran while one was open for 1% -> 1% of each run, Pallas kernels for 0% -> 0%
where the time goes in v1:
time: 455 us
  waiting for transfers between devices  174 us (38%)
  Pallas kernels  147 us (32%)
  blocking collectives  52.2 us (11%)
  matrix products  48.7 us (11%)
  between operations  13.9 us (3%)
  local copies, waits for them, and re-layouts  8.51 us (2%)
  other arithmetic  6.31 us (1%)
  starting transfers between devices  4.73 us (1%)
    pallas_call x1, Pallas kernels, expert_layer(): pl.pallas_call(partial(expert_kernel, n_ctx), out_shape=jax.ShapeDtypeStr...  147 us
    all_gather x1, waiting for transfers between devices, local(): lax.all_gather(head_out.reshape(tok_rows, -1), 'ctx', axis=0, tiled=True)  80.1 us
    reduce_scatter x1, waiting for transfers between devices, local(): lax.psum_scatter(jnp.dot(gathered, w_out, preferred_element_type=jnp.floa...  44.8 us
    all_to_all x1, blocking collectives, local(): lax.all_to_all(send_rows, 'exp', split_axis=0, concat_axis=0, tiled=True)  36.8 us
    all_to_all x1, waiting for transfers between devices, local(): lax.all_to_all(expert_out, 'exp', split_axis=0, concat_axis=0, tiled=True)  33.4 us
    all_gather x1, blocking collectives, local(): lax.all_gather(key_rope, 'ctx', axis=0, tiled=True)  15.3 us
    all_gather x1, waiting for transfers between devices, local(): lax.all_gather(kv_latent, 'ctx', axis=0, tiled=True)  15 us
    dot_general x1, matrix products, local(): jnp.dot(gathered, w_out, preferred_element_type=jnp.float32)  13.1 us
  transfers between devices with their start and end apart: 4, of which 4 were waited for; matrix products, arithmetic and copies ran while one was open for 1% of the time, Pallas kernels for 0%

profile of v1, /device:TPU:0, one launch (start us, length us, event | category | flops | bytes accessed | tf_op | source)
XLA Modules:
  0.0 454.9 jit_solution(11617372129481831412)
XLA Ops:
  7.2 0.0 all-gather.3.cloned.1.call-start
  7.2 0.7 all-gather.3.cloned.1.call-update
  7.9 0.0 all-gather.5.cloned.1.call-start
  8.0 2.1 copy.38
  10.0 15.3 %all_gather.10 = bf16[1024,64]{0,1:T(8,128)(2,1)S(1)} all-gather(bf16[256,64]{0,1:T(8,128)(2,1)} %param.15), channel_id=1, replica_groups=mesh['ctx'=4,'exp'=8] {'ctx'}, dimensions={0}, use_global_device_ids=true | all-gather | bytes 163840 | tf_op jit(solution)/shard_map/all_gather | solution.py:291
  25.4 0.2 iota_compare_fusion.1
  25.6 15.0 %all-gather.3.cloned.1.call-done = bf16[1024,512]{1,0:T(8,128)(2,1)} async-done(((bf16[256,512]{1,0:T(8,128)(2,1)}), bf16[1024,512]{1,0:T(8,128)(2,1)}) %all-gather.3.cloned.1.call-update) | async-done | bytes 1048592 | tf_op jit(solution)/shard_map/all_gather | solution.py:290
  40.6 10.5 %fusion.7 = f32[256,16,1024]{2,0,1:T(8,128)} fusion(bf16[16,128,512]{2,1,0:T(8,128)(2,1)S(1)} %copy-done, bf16[1024,512]{1,0:T(8,128)(2,1)} %all-gather.3.cloned.1.call-done, bf16[256,2048]{1,0:T(8,128)(2,1)} %param.12), kind=kOutput, calls=%fused_computation.10 | convolution fusion | flops 4833935360 | bytes 20971520 | tf_op jit(solution)/shard_map/ihc,jc->ihj/dot_general | solution.py:226
  51.1 8.1 %select_reduce_fusion = (f32[256,16]{0,1:T(8,128)S(1)}, f32[256,16,1024]{2,0,1:T(8,128)S(1)}) fusion(pred[256,1024]{1,0:T(8,128)(4,1)S(1)} %iota_compare_fusion.1, f32[256,16,1024]{2,0,1:T(8,128)} %fusion.7, bf16[256,16,64]{0,2,1:T(8,128)(2,1)} %bitcast.54, bf16[1024,64]{0,1:T(8,128)(2,1)S(1)} %all_gather.10), kind=kOutput, calls=%fused_computation.1 | convolution fusion | flops 553644032 | bytes 34488320 | tf_op jit(solution)/shard_map/ihr,jr->ihj/dot_general | solution.py:229
  59.3 5.7 %copy-done.2 = f32[256,16,1024]{2,0,1:T(8,128)} copy-done((f32[256,16,1024]{2,0,1:T(8,128)}, f32[256,16,1024]{2,0,1:T(8,128)S(1)}, u32[]{:S(2)}) %copy-start.2) | copy-done | bytes 16777240
  65.0 4.3 fusion
  69.3 11.9 %fusion.18 = bf16[16,256,128]{1,2,0:T(8,128)(2,1)} fusion(bf16[16,512,128]{2,1,0:T(8,128)(2,1)} %param.17, f32[256,16]{0,1:T(8,128)S(1)} %fusion, f32[256,16,1024]{2,0,1:T(8,128)} %copy-done.2, f32[256,16]{0,1:T(8,128)S(1)} %broadcast_maximum_fusion, pred[256,1024]{1,0:T(8,128)(4,1)S(1)} %iota_compare_fusion.1, bf16[1024,512]{1,0:T(8,128)(2,1)S(1)} %copy-done.5), kind=kOutput, calls=%fused_computation.21 | convolution fusion | flops 4849139712 | bytes 21266432 | tf_op jit(solution)/shard_map/ihc,hcv->ihv/dot_general | solution.py:296
  81.2 0.2 reduce-scatter.2.cloned.1.call-start
  81.4 80.1 %all-gather.5.cloned.1.call-done = bf16[1024,2048]{0,1:T(8,128)(2,1)} async-done(((bf16[256,2048]{0,1:T(8,128)(2,1)}), bf16[1024,2048]{0,1:T(8,128)(2,1)}) %all-gather.5.cloned.1.call-update) | async-done | bytes 4194320 | tf_op jit(solution)/shard_map/all_gather | solution.py:299
  161.6 13.1 %convolution_convert_fusion = bf16[1024,1792]{1,0:T(8,128)(2,1)} fusion(bf16[1024,2048]{0,1:T(8,128)(2,1)} %all-gather.5.cloned.1.call-done, bf16[2048,1792]{1,0:T(8,128)(2,1)} %param.18), kind=kOutput, calls=%fused_computation.14 | convolution fusion | flops 7518027776 | bytes 15204352 | tf_op jit(solution)/shard_map/dot_general | solution.py:302
  174.8 0.1 copy.40
  174.9 0.1 eq.42
  175.0 0.1 eq.38
  175.1 1.1 reduce-window.6
  176.2 0.2 slice_reduce_fusion
  176.5 0.1 fusion.32
  176.6 0.1 reduce_sum.43
  176.7 0.1 copy.42
  176.8 0.3 convert_reduce_fusion
  177.1 44.8 %reduce-scatter.2.cloned.1.call-done = bf16[128,1792]{1,0:T(8,128)(2,1)} async-done(((bf16[1024,1792]{1,0:T(8,128)(2,1)}), bf16[128,1792]{1,0:T(8,128)(2,1)}) %reduce-scatter.2.cloned.1.call-update) | async-done | bytes 458768 | tf_op jit(solution)/shard_map/reduce_scatter | solution.py:301
  221.8 1.9 convolution_convert_fusion.1
  223.7 36.8 %all_to_all.10 = bf16[8,96,1792]{2,1,0:T(8,128)(2,1)} all-to-all(bf16[8,96,1792]{2,1,0:T(8,128)(2,1)S(1)} %bitcast.51), channel_id=1, replica_groups=mesh['ctx'=4,'exp'=8] {'exp'}, dimensions={0} | all-to-all | bytes 5505024 | tf_op jit(solution)/shard_map/all_to_all | solution.py:327
  260.6 146.6 %expert_layer.1 = bf16[768,1792]{1,0:T(8,128)(2,1)} custom-call(bf16[768,1792]{1,0:T(8,128)(2,1)} %bitcast.53, bf16[1792,2048]{1,0:T(8,128)(2,1)} %bitcast.56, bf16[1792,2048]{1,0:T(8,128)(2,1)} %bitcast.57, bf16[2048,1792]{1,0:T(8,128)(2,1)} %bitcast.58), custom_call_target="tpu_custom_call" | custom-call | flops 16911433728 | bytes 22020096 | tf_op jit(solution)/shard_map/expert_layer/pallas_call | solution.py:194
  407.1 4.4 all-to-all-start.1
  411.6 0.2 fusion.28
  411.8 33.4 %all-to-all-done.1 = bf16[8,96,1792]{2,1,0:T(8,128)(2,1)} async-done(((bf16[8,96,1792]{2,1,0:T(8,128)(2,1)}), bf16[8,96,1792]{2,1,0:T(8,128)(2,1)}, u32[]{:S(2)}, u32[]{:S(2)}) %all-to-all-start.1) | async-done | bytes 2752544 | tf_op jit(solution)/shard_map/all_to_all | solution.py:333
  445.3 3.1 convolution_convert_fusion.2
  (19 shorter events, 0.1 us)
Async XLA Ops:
  7.2 33.4 %copy-start = (bf16[16,128,512]{2,1,0:T(8,128)(2,1)S(1)}, bf16[16,128,512]{2,1,0:T(8,128)(2,1)}, u32[]{:S(2)}) copy-start(bf16[16,128,512]{2,1,0:T(8,128)(2,1)} %param.16) | copy-start | bytes 6291460
  7.2 33.4 %all-gather.3.cloned.1.call-start = ((), (), s32[]{:S(2)}) async-start(), calls=%async_computation.3 | async-start | bytes 1310720 | tf_op jit(solution)/shard_map/all_gather | solution.py:290
  7.9 153.7 %all-gather.5.cloned.1.call-start = ((), (), s32[]{:S(2)}) async-start(), calls=%async_computation.4 | async-start | bytes 5242880 | tf_op jit(solution)/shard_map/all_gather | solution.py:299
  59.2 5.7 %copy-start.2 = (f32[256,16,1024]{2,0,1:T(8,128)}, f32[256,16,1024]{2,0,1:T(8,128)S(1)}, u32[]{:S(2)}) copy-start(f32[256,16,1024]{2,0,1:T(8,128)S(1)} %get-tuple-element.3) | copy-start | bytes 50331652
  65.0 4.3 copy-start.5
  81.2 93.5 %copy-start.3 = (s32[128,4]{0,1:T(4,128)S(1)}, s32[128,4]{0,1:T(4,128)}, u32[]{:S(2)}) copy-start(s32[128,4]{0,1:T(4,128)} %param.22) | copy-start | bytes 6148
  81.2 140.6 %reduce-scatter.2.cloned.1.call-start = ((), (), s32[]{:S(2)}) async-start(), calls=%async_computation.5 | async-start | bytes 4128768 | tf_op jit(solution)/shard_map/reduce_scatter | solution.py:301
  260.6 151.0 %copy-start.4 = (bf16[128,4]{0,1:T(4,128)(2,1)S(1)}, bf16[128,4]{0,1:T(4,128)(2,1)}, u32[]{:S(2)}) copy-start(bf16[128,4]{0,1:T(4,128)(2,1)} %param.23) | copy-start | bytes 3076
  260.6 187.8 %copy-start.1 = (bf16[16,128,512]{2,1,0:T(8,128)(2,1)S(1)}, bf16[16,128,512]{2,1,0:T(8,128)(2,1)}, u32[]{:S(2)}) copy-start(bf16[16,128,512]{2,1,0:T(8,128)(2,1)} %param.16) | copy-start | bytes 6291460
  407.1 38.1 %all-to-all-start.1 = ((bf16[8,96,1792]{2,1,0:T(8,128)(2,1)}), bf16[8,96,1792]{2,1,0:T(8,128)(2,1)}, u32[]{:S(2)}, u32[]{:S(2)}) async-start(bf16[8,96,1792]{2,1,0:T(8,128)(2,1)} %bitcast.52), calls=%async_computation.2 | async-start | bytes 5505024 | tf_op jit(solution)/shard_map/all_to_all | solution.py:333
Sparse Core Ops, SparseCore 0:
  9.6 30.9 all-gather.2
  81.3 80.2 all-gather.4
  174.9 46.9 reduce-scatter.1

commit v2 on v1

--- a/solution.py
+++ b/solution.py
@@ -219,30 +219,401 @@
         name="expert_layer",
     )(rows_in, gate_w, up_w, down_w)
 
-
-def score_block(running, pieces, key_start, query_latent, query_rope, query_pos, score_scale):
-    running_max, running_sum, running_acc = running
-    latent_piece, rope_piece = pieces
-    scores = jnp.einsum(
-        "ihc,jc->ihj", query_latent, latent_piece, preferred_element_type=jnp.float32
-    )
-    scores = scores + jnp.einsum(
-        "ihr,jr->ihj", query_rope, rope_piece, preferred_element_type=jnp.float32
-    )
-    scores = scores * score_scale
-    key_pos = jnp.arange(latent_piece.shape[0], dtype=jnp.int32)
-    allowed = (key_pos[None, :] <= query_pos[:, None])[:, None, :]
-    block_max = jnp.max(jnp.where(allowed, scores, NEG_FILL), axis=2)
-    new_max = jnp.maximum(running_max, block_max)
-    exp_terms = jnp.where(allowed, jnp.exp(scores - new_max[:, :, None]), 0.0)
-    new_sum = jnp.sum(exp_terms, axis=2)
-    update = jnp.einsum(
-        "ihj,jc->ihc",
-        exp_terms.astype(jnp.bfloat16),
-        latent_piece,
-        preferred_element_type=jnp.float32,
-    )
-    return (new_max, new_sum, update)
+def attend_kernel(
+    n_ctx, score_scale, q_nope, q_rope, kv, w_uk, w_uv, wo_hbm, out, keys, queries, heads, acc, wo,
+    w_sem, kv_send, kv_recv, core_send, core_recv, h_send, h_recv,
+):
+    p = lax.axis_index("ctx")
+    e = lax.axis_index("exp")
+    last = n_ctx - 1
+    half = e % 2
+    sibling = e + 1 - 2 * half
+    tok = q_nope.shape[0]
+    part = tok // 2
+    head_count, nope, lat = w_uk.shape
+    vhead = w_uv.shape[2]
+    rope2 = kv.shape[1] - lat
+    pairs = head_count // 2
+    total = keys.shape[0]
+
+    load = pltpu.make_async_copy(wo_hbm, wo, w_sem)
+    load.start()
+
+    barrier = pltpu.get_barrier_semaphore()
+    for o in range(n_ctx):
+
+        @pl.when(p != o)
+        def _():
+            pl.semaphore_signal(barrier, inc=1, device_id={"ctx": o}, device_id_type=MESH)
+
+    pl.semaphore_signal(barrier, inc=1, device_id={"exp": sibling}, device_id_type=MESH)
+    pl.semaphore_wait(barrier, n_ctx)
+
+    def kv_copy(i):
+        return pltpu.make_async_remote_copy(
+            src_ref=kv.at[pl.ds(pl.multiple_of(half * part, part), part)],
+            dst_ref=keys.at[pl.ds(pl.multiple_of(p * tok + half * part, part), part)],
+            send_sem=kv_send.at[i],
+            recv_sem=kv_recv.at[p],
+            device_id={"ctx": jnp.minimum(p + 1 + i, last)},
+            device_id_type=MESH,
+        )
+
+    def kv_arrival(o):
+        at = pl.ds(pl.multiple_of(o * tok + half * part, part), part)
+        return pltpu.make_async_remote_copy(
+            src_ref=keys.at[at],
+            dst_ref=keys.at[at],
+            send_sem=kv_send.at[0],
+            recv_sem=kv_recv.at[o],
+            device_id={"ctx": jnp.maximum(p - 1, 0)},
+            device_id_type=MESH,
+        )
+
+    def core_copy(o, side):
+        at = pl.ds(pl.multiple_of(o * tok + side * part, part), part)
+        return pltpu.make_async_remote_copy(
+            src_ref=keys.at[at],
+            dst_ref=keys.at[at],
+            send_sem=core_send.at[o],
+            recv_sem=core_recv.at[o],
+            device_id={"exp": sibling},
+            device_id_type=MESH,
+        )
+
+    for i in range(last):
+
+        @pl.when(p + 1 + i <= last)
+        def _():
+            kv_copy(i).start()
+
+    for o in range(n_ctx):
+
+        @pl.when(p == o)
+        def _():
+            keys[pl.ds(o * tok, tok), :] = kv[...]
+
+        @pl.when(p < o)
+        def _():
+            keys[pl.ds(o * tok, tok), :] = jnp.zeros((tok, keys.shape[1]), keys.dtype)
+
+    @pl.loop(0, pairs)
+    def _(s):
+        rope = q_rope[:, pl.ds(pl.multiple_of(s * rope2, rope2), rope2)]
+        lane = lax.broadcasted_iota(jnp.int32, rope.shape, 1)
+        for a in range(2):
+            h = 2 * s + a
+            queries[h, :, pl.ds(0, lat)] = jnp.dot(
+                q_nope[:, pl.ds(pl.multiple_of(h * nope, nope), nope)],
+                w_uk[h],
+                preferred_element_type=jnp.float32,
+            ).astype(queries.dtype)
+            own = (lane < rope2 // 2) if a == 0 else (lane >= rope2 // 2)
+            queries[h, :, pl.ds(lat, rope2)] = jnp.where(own, rope, jnp.zeros_like(rope))
+
+    for o in reversed(range(last)):
+
+        @pl.when(o < p)
+        def _():
+            kv_arrival(o).wait_recv()
+            core_copy(o, half).start()
+
+    for o in reversed(range(last)):
+
+        @pl.when(o < p)
+        def _():
+            core_copy(o, 1 - half).wait_recv()
+
+    def head_copy(way, o, t):
+        at = pl.ds(pl.multiple_of(o * tok, tok), tok)
+        cols = pl.ds(pl.multiple_of((t % 2) * 2 * vhead, 2 * vhead), 2 * vhead)
+        there = jnp.minimum(p + 1, last) if way == 0 else jnp.maximum(p - 1, 0)
+        return pltpu.make_async_remote_copy(
+            src_ref=heads.at[t // 2, at, cols],
+            dst_ref=heads.at[t // 2, at, cols],
+            send_sem=h_send.at[(way * n_ctx + o) * pairs + t],
+            recv_sem=h_recv.at[o * pairs + t],
+            device_id={"ctx": there},
+            device_id_type=MESH,
+        )
+
+    query_pos = p * tok + lax.broadcasted_iota(jnp.int32, (tok, total), 0)
+    key_pos = lax.broadcasted_iota(jnp.int32, (tok, total), 1)
+
+    @pl.loop(0, pairs + n_ctx - 2)
+    def _(s):
+        @pl.when(s < pairs)
+        def _():
+            for a in range(2):
+                h = 2 * s + a
+                scores = lax.dot_general(
+                    queries[h],
+                    keys[...],
+                    (((1,), (1,)), ((), ())),
+                    preferred_element_type=jnp.float32,
+                )
+                scores = jnp.where(key_pos <= query_pos, scores * score_scale, NEG_FILL)
+                terms = jnp.exp(scores - jnp.max(scores, axis=1, keepdims=True))
+                sums = jnp.sum(terms, axis=1, keepdims=True)
+                mixed = jnp.dot(
+                    terms.astype(jnp.bfloat16),
+                    keys[:, pl.ds(0, lat)],
+                    preferred_element_type=jnp.float32,
+                )
+                latent_out = (mixed / sums).astype(jnp.bfloat16)
+                cols = pl.ds(
+                    pl.multiple_of((s % 2) * 2 * vhead + a * vhead, vhead), vhead
+                )
+                heads[s // 2, pl.ds(pl.multiple_of(p * tok, tok), tok), cols] = jnp.dot(
+                    latent_out, w_uv[h], preferred_element_type=jnp.float32
+                ).astype(heads.dtype)
+
+            @pl.when(p < last)
+            def _():
+                head_copy(0, p, s).start()
+
+            @pl.when(p > 0)
+            def _():
+                head_copy(1, p, s).start()
+
+        for k in range(1, n_ctx - 1):
+            t = s - k
+
+            @pl.when((t >= 0) & (t < pairs) & (p - k >= 0) & (p < last))
+            def _():
+                head_copy(0, p - k, t).wait_recv()
+                head_copy(0, p - k, t).start()
+
+            @pl.when((t >= 0) & (t < pairs) & (p + k <= last) & (p > 0))
+            def _():
+                head_copy(1, p + k, t).wait_recv()
+                head_copy(1, p + k, t).start()
+
+    load.wait()
+    width = out.shape[1]
+    tile = 256 if width % 256 == 0 else 128
+    depth = 4 * vhead
+    groups = pairs // 2
+    for g in range(groups):
+        for t in (2 * g, 2 * g + 1):
+
+            @pl.when(p == last)
+            def _():
+                for o in range(last):
+                    head_copy(0, o, t).wait_recv()
+
+            @pl.when(p == 0)
+            def _():
+                for o in range(1, n_ctx):
+                    head_copy(1, o, t).wait_recv()
+
+        @pl.loop(0, width // tile)
+        def _(c):
+            cols = pl.ds(pl.multiple_of(c * tile, tile), tile)
+            term = jnp.dot(
+                heads[g], wo[pl.ds(g * depth, depth), cols], preferred_element_type=jnp.float32
+            )
+            if g > 0:
+                term = acc[:, cols] + term
+            if g < groups - 1:
+                acc[:, cols] = term
+            else:
+                out[:, cols] = term.astype(out.dtype)
+
+    for i in range(last):
+
+        @pl.when(p + 1 + i <= last)
+        def _():
+            kv_copy(i).wait_send()
+
+        @pl.when(i < p)
+        def _():
+            core_copy(i, half).wait_send()
+
+    @pl.loop(0, pairs)
+    def _(t):
+        for o in range(n_ctx):
+
+            @pl.when((o <= p) & (p < last))
+            def _():
+                head_copy(0, o, t).wait_send()
+
+            @pl.when((o >= p) & (p > 0))
+            def _():
+                head_copy(1, o, t).wait_send()
+
+
+def attend(q_nope, q_rope, kv, w_uk, w_uv, w_out, score_scale):
+    n_ctx = lax.axis_size("ctx")
+    tok = q_nope.shape[0]
+    head_count, nope, lat = w_uk.shape
+    vhead = w_uv.shape[2]
+    pairs = head_count // 2
+    total = n_ctx * tok
+    width = w_out.shape[1]
+    dma = pltpu.SemaphoreType.DMA
+    return pl.pallas_call(
+        partial(attend_kernel, n_ctx, score_scale),
+        out_shape=jax.ShapeDtypeStruct((total, width), jnp.bfloat16),
+        in_specs=[pl.BlockSpec(memory_space=pltpu.VMEM)] * 5
+        + [pl.BlockSpec(memory_space=pl.ANY)],
+        out_specs=pl.BlockSpec(memory_space=pltpu.VMEM),
+        scratch_shapes=[
+            pltpu.VMEM((total, kv.shape[1]), jnp.bfloat16),
+            pltpu.VMEM((head_count, tok, kv.shape[1]), jnp.bfloat16),
+            pltpu.VMEM((pairs // 2, total, 4 * vhead), jnp.bfloat16),
+            pltpu.VMEM((total, width), jnp.float32),
+            pltpu.VMEM(w_out.shape, jnp.bfloat16),
+            dma,
+            dma((n_ctx,)),
+            dma((n_ctx,)),
+            dma((n_ctx,)),
+            dma((n_ctx,)),
+            dma((2 * n_ctx * pairs,)),
+            dma((n_ctx * pairs,)),
+        ],
+        compiler_params=pltpu.CompilerParams(
+            collective_id=1, has_side_effects=True, vmem_limit_bytes=56 * 1024 * 1024
+        ),
+        cost_estimate=pl.CostEstimate(
+            flops=2 * total * width * w_out.shape[0],
+            bytes_accessed=2 * w_out.size,
+            transcendentals=head_count * tok * total,
+        ),
+        name="attend",
+    )(q_nope, q_rope, kv, w_uk, w_uv, w_out)
+
+
+def exp_kernel(bits, cols, spread, *refs):
+    refs = list(refs)
+    mine = refs.pop(0)
+    extra = refs.pop(0) if spread else None
+    out = refs.pop(0)
+    every = refs.pop(0) if spread else None
+    sums = [[refs.pop(0) for _ in range(bits)] for _ in cols]
+    came = [[refs.pop(0) for _ in range(bits)] for _ in cols]
+    rs_send, rs_recv = refs.pop(0), refs.pop(0)
+    if spread:
+        ag_send, ag_recv = refs.pop(0), refs.pop(0)
+
+    e = lax.axis_index("exp")
+    bit = [(e // (1 << b)) % 2 for b in range(bits)]
+    partner = [e + (1 - 2 * bit[b]) * (1 << b) for b in range(bits)]
+    orders = [list(range(bits)), [0] + list(range(bits - 1, 0, -1))]
+
+    barrier = pltpu.get_barrier_semaphore()
+    for b in range(bits):
+        pl.semaphore_signal(barrier, inc=1, device_id={"exp": partner[b]}, device_id_type=MESH)
+    pl.semaphore_wait(barrier, bits)
+
+    def place(free, at):
+        return tuple(at.get(b, slice(None)) for b in free)
+
+    copies = []
+    for j in range(bits):
+        stage = []
+        for f, (start, size) in enumerate(cols):
+            b = orders[f][j]
+            free = [x for x in range(bits - 1, -1, -1) if x not in orders[f][:j]]
+            there = place(free, {b: 1 - bit[b]})
+            if j == 0:
+                src = mine.at[there + (slice(None), pl.ds(start, size))]
+            else:
+                src = sums[f][j - 1].at[there]
+            copy = pltpu.make_async_remote_copy(
+                src_ref=src,
+                dst_ref=came[f][j],
+                send_sem=rs_send.at[f * bits + j],
+                recv_sem=rs_recv.at[f * bits + j],
+                device_id={"exp": partner[b]},
+                device_id_type=MESH,
+            )
+            copy.start()
+            stage.append(copy)
+        for f, (start, size) in enumerate(cols):
+            b = orders[f][j]
+            free = [x for x in range(bits - 1, -1, -1) if x not in orders[f][:j]]
+            here = place(free, {b: bit[b]})
+            stage[f].wait_recv()
+            if j == 0:
+                own = mine[here + (slice(None), pl.ds(start, size))]
+            else:
+                own = sums[f][j - 1][here]
+            sums[f][j][...] = (
+                own.astype(jnp.float32) + came[f][j][...].astype(jnp.float32)
+            ).astype(jnp.bfloat16)
+        copies += stage
+
+    spot = tuple(bit[b] for b in range(bits - 1, -1, -1))
+    for f, (start, size) in enumerate(cols):
+        out[:, pl.ds(start, size)] = sums[f][bits - 1][...]
+        if spread:
+            every[spot + (slice(None), pl.ds(start, size))] = sums[f][bits - 1][...]
+    if spread:
+        width = mine.shape[-1]
+        more = extra.shape[-1]
+        every[spot + (slice(None), pl.ds(width, more))] = extra[...]
+        for j in reversed(range(bits)):
+            stage = []
+            for f, (start, size) in enumerate(cols):
+                size = size + (more if f == 1 else 0)
+                at = place(range(bits - 1, -1, -1), {b: bit[b] for b in orders[f][: j + 1]})
+                block = every.at[at + (slice(None), pl.ds(start, size))]
+                copy = pltpu.make_async_remote_copy(
+                    src_ref=block,
+                    dst_ref=block,
+                    send_sem=ag_send.at[f * bits + j],
+                    recv_sem=ag_recv.at[f * bits + j],
+                    device_id={"exp": partner[orders[f][j]]},
+                    device_id_type=MESH,
+                )
+                copy.start()
+                stage.append(copy)
+            for copy in stage:
+                copy.wait_recv()
+            copies += stage
+    for copy in copies:
+        copy.wait_send()
+
+
+def exp_sum(rows_in, extra, collective_id):
+    n_exp = lax.axis_size("exp")
+    bits = n_exp.bit_length() - 1
+    total, width = rows_in.shape
+    rows = total // n_exp
+    spread = extra is not None
+    first = (width // 2 + 127) // 128 * 128
+    cols = ((0, first), (first, width - first))
+    vmem = pl.BlockSpec(memory_space=pltpu.VMEM)
+    shapes = []
+    for _ in range(2):
+        for _, size in cols:
+            for j in range(bits):
+                shapes.append(pltpu.VMEM((2,) * (bits - 1 - j) + (rows, size), jnp.bfloat16))
+    shapes += [pltpu.SemaphoreType.DMA((2 * bits,))] * (4 if spread else 2)
+    out_shape = [jax.ShapeDtypeStruct((rows, width), jnp.bfloat16)]
+    operands = [rows_in.reshape((2,) * bits + (rows, width))]
+    if spread:
+        wide = width + extra.shape[1]
+        out_shape.append(jax.ShapeDtypeStruct((2,) * bits + (rows, wide), jnp.bfloat16))
+        operands.append(extra)
+    got = pl.pallas_call(
+        partial(exp_kernel, bits, cols, spread),
+        out_shape=out_shape,
+        in_specs=[vmem] * len(operands),
+        out_specs=[vmem] * len(out_shape),
+        scratch_shapes=shapes,
+        compiler_params=pltpu.CompilerParams(
+            collective_id=collective_id, has_side_effects=True, vmem_limit_bytes=40 * 1024 * 1024
+        ),
+        cost_estimate=pl.CostEstimate(
+            flops=2 * total * width, bytes_accessed=4 * total * width, transcendentals=0
+        ),
+        name="exp_sum_spread" if spread else "exp_sum",
+    )(*operands)
+    if spread:
+        return got[0], got[1].reshape(total, wide)
+    return got[0]
 
 
 def local(
@@ -259,82 +630,45 @@
     route_ids,
     route_gates,
 ):
-    tok_rows = q_nope.shape[0]
-    head_count, nope_size, latent_size = w_uk.shape
+    nope_size = w_uk.shape[1]
     rope_size = key_rope.shape[1]
-    score_scale = 1.0 / math.sqrt(nope_size + rope_size)
-    ctx_here = lax.axis_index("ctx")
-    query_pos = ctx_here * tok_rows + jnp.arange(tok_rows, dtype=jnp.int32)
-    query_latent = jnp.einsum(
-        "ihd,hdc->ihc",
-        q_nope.reshape(tok_rows, head_count, nope_size),
-        w_uk,
+    n_exp = lax.axis_size("exp")
+    keys = jnp.concatenate([kv_latent, key_rope, key_rope], axis=1)
+    partial_out = attend(
+        q_nope, q_rope, keys, w_uk, w_uv, w_out, 1.0 / math.sqrt(nope_size + rope_size)
+    )
+    out_rows, top_count = route_ids.shape
+    routing = jnp.concatenate([route_ids.astype(jnp.bfloat16), route_gates], axis=1)
+    routing = jnp.pad(routing, ((0, 0), (0, 128 - 2 * top_count)))
+    attn_out, gathered = exp_sum(partial_out, routing, 2)
+    total, width = partial_out.shape
+    capacity = 3 * out_rows * top_count // (2 * n_exp)
+    slot_total = n_exp * capacity
+    ids = gathered[:, width : width + top_count].astype(jnp.float32)
+    gates = gathered[:, width + top_count : width + 2 * top_count].astype(jnp.float32)
+    named = ids == lax.axis_index("exp").astype(jnp.float32)
+    chosen = jnp.any(named, axis=1)
+    gate = jnp.sum(jnp.where(named, gates, 0.0), axis=1)
+    below = jnp.tril(jnp.ones((out_rows, out_rows), jnp.bfloat16), -1)
+    ranks = lax.dot_general(
+        chosen.astype(jnp.bfloat16).reshape(n_exp, out_rows),
+        below,
+        (((1,), (1,)), ((), ())),
         preferred_element_type=jnp.float32,
+    ).astype(jnp.int32)
+    slots = ranks + capacity * jnp.arange(n_exp, dtype=jnp.int32)[:, None]
+    slots = jnp.where(chosen, slots.reshape(total), -1)
+    slot_range = jnp.arange(slot_total, dtype=jnp.int32)
+    placing = (slots[None, :] == slot_range[:, None]).astype(jnp.bfloat16)
+    arrived = jnp.dot(
+        placing, gathered[:, :width], preferred_element_type=jnp.float32
     ).astype(jnp.bfloat16)
-    query_rope = q_rope.reshape(tok_rows, head_count, rope_size)
-    initial = (
-        jnp.full((tok_rows, head_count), NEG_FILL, jnp.float32),
-        jnp.zeros((tok_rows, head_count), jnp.float32),
-        jnp.zeros((tok_rows, head_count, latent_size), jnp.float32),
-    )
-    step_fn = partial(
-        score_block,
-        query_latent=query_latent,
-        query_rope=query_rope,
-        query_pos=query_pos,
-        score_scale=score_scale,
-    )
-    attended = step_fn(
-        initial,
-        (
-            lax.all_gather(kv_latent, "ctx", axis=0, tiled=True),
-            lax.all_gather(key_rope, "ctx", axis=0, tiled=True),
-        ),
-        jnp.int32(0),
-    )
-    latent_out = (attended[2] / attended[1][:, :, None]).astype(jnp.bfloat16)
-    head_out = jnp.einsum(
-        "ihc,hcv->ihv", latent_out, w_uv, preferred_element_type=jnp.float32
+    expert_out = expert_layer(arrived, w_gate[0], w_up[0], w_down[0])
+    weighting = jnp.where(slots[:, None] == slot_range[None, :], gate[:, None], 0.0)
+    share = jnp.dot(
+        weighting.astype(jnp.bfloat16), expert_out, preferred_element_type=jnp.float32
     ).astype(jnp.bfloat16)
-    gathered = lax.all_gather(head_out.reshape(tok_rows, -1), "ctx", axis=0, tiled=True)
-    out_rows = gathered.shape[0] // lax.axis_size("exp")
-    attn_out = lax.psum_scatter(
-        jnp.dot(gathered, w_out, preferred_element_type=jnp.float32).astype(jnp.bfloat16),
-        "exp",
-        scatter_dimension=0,
-        tiled=True,
-    )
-    feature_cols = attn_out.shape[1]
-    top_count = route_ids.shape[1]
-    expert_count = lax.axis_size("exp") * w_gate.shape[0]
-    capacity = 3 * out_rows * top_count // (2 * expert_count)
-    slot_total = expert_count * capacity
-    flat_ids = route_ids.reshape(-1)
-    onehot = (flat_ids[:, None] == jnp.arange(expert_count, dtype=jnp.int32)[None, :]).astype(
-        jnp.int32
-    )
-    earlier = jnp.cumsum(onehot, axis=0) - onehot
-    slot_ids = jnp.sum(earlier * onehot, axis=1)
-    targets = (flat_ids * capacity + slot_ids).reshape(out_rows, top_count)
-    slot_range = jnp.arange(slot_total, dtype=jnp.int32)
-    hits = targets[:, :, None] == slot_range[None, None, :]
-    placing = jnp.sum(hits.astype(jnp.float32), axis=1).astype(jnp.bfloat16).T
-    send_rows = jnp.dot(placing, attn_out, preferred_element_type=jnp.float32).astype(jnp.bfloat16)
-    send_rows = send_rows.reshape(expert_count, capacity, feature_cols)
-    weighting = jnp.sum(
-        jnp.where(hits, route_gates[:, :, None], jnp.zeros((), jnp.bfloat16)), axis=1
-    )
-    arrived = lax.all_to_all(send_rows, "exp", split_axis=0, concat_axis=0, tiled=True)
-    source_count = arrived.shape[0]
-    item_count = arrived.shape[1]
-    flat_rows = arrived.reshape(source_count * item_count, feature_cols)
-    expert_out = expert_layer(flat_rows, w_gate[0], w_up[0], w_down[0])
-    expert_out = expert_out.reshape(source_count, item_count, feature_cols)
-    returned = lax.all_to_all(expert_out, "exp", split_axis=0, concat_axis=0, tiled=True)
-    moe_out = jnp.dot(
-        weighting, returned.reshape(slot_total, feature_cols), preferred_element_type=jnp.float32
-    ).astype(jnp.bfloat16)
-    return (attn_out, moe_out)
+    return (attn_out, exp_sum(share, None, 3))
 
 
 def solution(mesh):

time: 455 us -> 336 us (0.74)
  waiting for transfers between devices: 174 us -> 0 us
  Pallas kernels: 147 us -> 317 us
  blocking collectives: 52.2 us -> 0 us
  matrix products: 48.7 us -> 9.97 us
  between operations: 13.9 us -> 0.71 us
  starting transfers between devices: 4.73 us -> 0 us
    pallas_call x0 -> x3, Pallas kernels: none -> 169 us  [the longest x1 97.8 us: attend(): pl.pallas_call(partial(attend_kernel, n_ctx, score_scale), out_shape=jax....]
    all_gather x2 -> x0, waiting for transfers between devices: 95.1 us -> none  [the longest x1 80.1 us: local(): lax.all_gather(head_out.reshape(tok_rows, -1), 'ctx', axis=0, tiled=True)]
    reduce_scatter x1 -> x0, waiting for transfers between devices: 44.8 us -> none  [local(): lax.psum_scatter(jnp.dot(gathered, w_out, preferred_element_type=jnp.floa...]
    dot_general x6 -> x3, matrix products: 48.7 us -> 9.97 us  [the longest x1 5.37 us: local(): jnp.dot(weighting.astype(jnp.bfloat16), expert_out, preferred_element_typ...]
    all_to_all x1 -> x0, blocking collectives: 36.8 us -> none  [local(): lax.all_to_all(send_rows, 'exp', split_axis=0, concat_axis=0, tiled=True)]
    all_to_all x1 -> x0, waiting for transfers between devices: 33.4 us -> none  [local(): lax.all_to_all(expert_out, 'exp', split_axis=0, concat_axis=0, tiled=True)]
    all_gather x1 -> x0, blocking collectives: 15.3 us -> none  [local(): lax.all_gather(key_rope, 'ctx', axis=0, tiled=True)]
    reduce_sum x4 -> x1, other arithmetic: 4.89 us -> 0.27 us  [local(): gate = jnp.sum(jnp.where(named, gates, 0.0), axis=1)]
  transfers between devices with their start and end apart: 4 -> 0, of which waited for: 4 -> 0; matrix products, arithmetic and copies ran while one was open for 1% -> 0% of each run, Pallas kernels for 0% -> 0%
where the time goes in v2:
time: 336 us
  Pallas kernels  317 us (94%)
  matrix products  9.97 us (3%)
  local copies, waits for them, and re-layouts  4.58 us (1%)
  other arithmetic  3.64 us (1%)
    pallas_call x1, Pallas kernels, expert_layer(): pl.pallas_call(partial(expert_kernel, n_ctx), out_shape=jax.ShapeDtypeStr...  148 us
    pallas_call x1, Pallas kernels, attend(): pl.pallas_call(partial(attend_kernel, n_ctx, score_scale), out_shape=jax....  97.8 us
    pallas_call x2, Pallas kernels, exp_sum(): pl.pallas_call(partial(exp_kernel, bits, cols, spread), out_shape=out_sha...  70.9 us

profile of v2, /device:TPU:0, one launch (start us, length us, event | category | flops | bytes accessed | tf_op | source)
XLA Modules:
  0.0 335.6 jit_solution(3849023657154788748)
XLA Ops:
  0.7 0.7 convert_element_type.28
  1.3 0.7 pad_maximum_fusion.1
  2.0 0.1 copy.20
  2.2 0.9 copy.18
  3.0 1.8 pad_maximum_fusion.kv
  4.8 97.8 %attend.1 = bf16[1024,1792]{1,0:T(8,128)(2,1)} custom-call(bf16[256,2048]{1,0:T(8,128)(2,1)} %q_nope.1, bf16[256,1024]{1,0:T(8,128)(2,1)} %q_rope.1, bf16[256,640]{1,0:T(8,128)(2,1)} %pad_maximum_fusion.kv, bf16[16,128,512]{2,1,0:T(8,128)(2,1)} %w_uk.1, bf16[16,512,128]{2,1,0:T(8,128)(2,1)} %w_uv.1, bf16[2048,1792]{1,0:T(8,128)(2,1)} %wo_hbm.1), custom_call_target="tpu_custom_call" | custom-call | flops 7516192768 | bytes 7340032 | tf_op jit(solution)/shard_map/attend/pallas_call | solution.py:455
  102.6 0.0 copy-start
  102.6 2.0 copy-done
  104.6 47.4 %exp_sum_spread.1 = (bf16[128,1792]{1,0:T(8,128)(2,1)S(1)}, bf16[2,2,2,128,1920]{4,3,2,1,0:T(8,128)(2,1)S(1)}) custom-call(bf16[2,2,2,128,1792]{4,3,2,1,0:T(8,128)(2,1)S(1)} %bitcast.14, bf16[128,128]{1,0:T(8,128)(2,1)S(1)} %pad.4.refs_1_), custom_call_target="tpu_custom_call" | custom-call | flops 3670016 | bytes 7340032 | tf_op jit(solution)/shard_map/exp_sum_spread/pallas_call | solution.py:600
  152.1 0.2 fusion.17
  152.3 0.3 select_reduce_fusion
  152.6 0.2 fusion.11
  152.8 4.4 %fusion.2.x = bf16[768,1792]{1,0:T(8,128)(2,1)} fusion(bf16[1024,1920]{1,0:T(8,128)(2,1)S(1)} %bitcast.18, s32[1024]{0:T(1024)S(1)} %fusion.11), kind=kOutput, calls=%fused_computation.3 | convolution fusion | flops 2820734976 | bytes 6426624 | tf_op jit(solution)/shard_map/dot_general | solution.py:663
  157.2 148.1 %expert_layer.1 = bf16[768,1792]{1,0:T(8,128)(2,1)} custom-call(bf16[768,1792]{1,0:T(8,128)(2,1)} %fusion.2.x, bf16[1792,2048]{1,0:T(8,128)(2,1)} %bitcast.19, bf16[1792,2048]{1,0:T(8,128)(2,1)} %bitcast.20, bf16[2048,1792]{1,0:T(8,128)(2,1)} %bitcast.21), custom_call_target="tpu_custom_call" | custom-call | flops 16911433728 | bytes 22020096 | tf_op jit(solution)/shard_map/expert_layer/pallas_call | solution.py:194
  305.2 5.4 %convolution_convert_fusion = bf16[1024,1792]{1,0:T(8,128)(2,1)S(1)} fusion(bf16[768,1792]{1,0:T(8,128)(2,1)} %expert_layer.1, bf16[1024]{0:T(1024)(128)(2,1)S(1)} %select_reduce_fusion, s32[1024]{0:T(1024)S(1)} %fusion.11), kind=kOutput, calls=%fused_computation | convolution fusion | flops 2821980160 | bytes 6428672 | tf_op jit(solution)/shard_map/dot_general | solution.py:668
  310.6 23.5 %exp_sum.1 = bf16[128,1792]{1,0:T(8,128)(2,1)S(1)} custom-call(bf16[2,2,2,128,1792]{4,3,2,1,0:T(8,128)(2,1)S(1)} %bitcast.15), custom_call_target="tpu_custom_call" | custom-call | flops 3670016 | bytes 7340032 | tf_op jit(solution)/shard_map/exp_sum/pallas_call | solution.py:600
  334.1 0.8 copy.23
  334.8 0.8 copy.24
  (3 shorter events, 0.0 us)
Async XLA Ops:
  102.6 2.0 copy-start

commit v3 on v2

--- a/solution.py
+++ b/solution.py
@@ -11,6 +11,8 @@
 NEG_FILL = -1e30
 MESH = pl.DeviceIdType.MESH
 CHUNK = 16
+SLACK = 2
+AHEAD = 3
 BLOCK = 128
 
 
@@ -28,10 +30,15 @@
     blocks = half // BLOCK
     tile = 512 if ff % 512 == 0 else ff
 
-    loads = [
-        pltpu.make_async_copy(src, dst, w_sem.at[i])
-        for i, (src, dst) in enumerate(((wg_hbm, wg), (wu_hbm, wu), (wd_hbm, wd)))
-    ]
+    tiles = ff // tile
+    loads = []
+    for c in range(tiles):
+        cols = pl.ds(c * tile, tile)
+        for src, dst in ((wg_hbm, wg), (wu_hbm, wu)):
+            loads.append(
+                pltpu.make_async_copy(src.at[:, cols], dst.at[:, cols], w_sem.at[len(loads)])
+            )
+    loads.append(pltpu.make_async_copy(wd_hbm, wd, w_sem.at[len(loads)]))
     for load in loads:
         load.start()
 
@@ -74,19 +81,21 @@
             device_id_type=MESH,
         )
 
+    def gate_up_tile(d, block, c):
+        at = pl.ds(pl.multiple_of(d * half + block * BLOCK, BLOCK), BLOCK)
+        base = pl.multiple_of(c * tile, tile)
+        above = pl.multiple_of(ff + c * tile, tile)
+        part[at, pl.ds(base, tile)] = jnp.dot(
+            x[at, :], wg[:, pl.ds(base, tile)], preferred_element_type=jnp.float32
+        ).astype(part.dtype)
+        part[at, pl.ds(above, tile)] = jnp.dot(
+            x[at, :], wu[:, pl.ds(base, tile)], preferred_element_type=jnp.float32
+        ).astype(part.dtype)
+
     def gate_up(d, block):
-        at = pl.ds(pl.multiple_of(d * half + block * BLOCK, BLOCK), BLOCK)
-
-        @pl.loop(0, ff // tile)
+        @pl.loop(0, tiles)
         def _(c):
-            base = pl.multiple_of(c * tile, tile)
-            above = pl.multiple_of(ff + c * tile, tile)
-            part[at, pl.ds(base, tile)] = jnp.dot(
-                x[at, :], wg[:, pl.ds(base, tile)], preferred_element_type=jnp.float32
-            ).astype(part.dtype)
-            part[at, pl.ds(above, tile)] = jnp.dot(
-                x[at, :], wu[:, pl.ds(base, tile)], preferred_element_type=jnp.float32
-            ).astype(part.dtype)
+            gate_up_tile(d, block, c)
 
     width = out.shape[1]
     down_tile = 256 if width % 256 == 0 else 128
@@ -102,19 +111,24 @@
             ).astype(out.dtype)
 
     first = (2 * p > last).astype(jnp.int32)
-    loads[0].wait()
-    loads[1].wait()
-    gate_up(first, 0)
-
-    @pl.loop(0, n + 2 * last)
+    for c in range(tiles):
+        loads[2 * c].wait()
+        loads[2 * c + 1].wait()
+        gate_up_tile(first, 0, c)
+
+    @pl.loop(0, n + 2 * last * SLACK)
     def _(s):
         for d in range(2):
             k = p if d == 0 else last - p
-            t = s - k
+            t = s - k * SLACK
 
             @pl.when((t >= 0) & (t < n))
             def _():
                 at = chunk_rows(d, t)
+
+                @pl.when((k == 0) & (t >= AHEAD))
+                def _():
+                    rs_copy(d, t - AHEAD, part).wait_send()
 
                 @pl.when(k == 0)
                 def _():
@@ -142,7 +156,7 @@
 
         for d in range(2):
             j = last - p if d == 0 else p
-            u = s - last - j
+            u = s - (last + j) * SLACK
 
             @pl.when((u >= 0) & (u < n))
             def _():
@@ -162,11 +176,11 @@
 
         @pl.when(s == last)
         def _():
-            loads[2].wait()
+            loads[-1].wait()
 
         for d in range(2):
             j = last - p if d == 0 else p
-            u = s - last - j
+            u = s - (last + j) * SLACK
 
             @pl.when((u >= 0) & (u < n) & (u % per == per - 1))
             def _():
@@ -177,7 +191,7 @@
         for d in range(2):
             k = p if d == 0 else last - p
 
-            @pl.when(k < last)
+            @pl.when((k < last) & ((k > 0) | (t >= n - AHEAD)))
             def _():
                 rs_copy(d, t, held).wait_send()
 
@@ -204,7 +218,7 @@
             pltpu.VMEM((rows, 2 * ff), jnp.bfloat16),
             pltpu.VMEM((rows, 2 * ff), jnp.bfloat16),
             pltpu.VMEM((rows, ff), jnp.bfloat16),
-            pltpu.SemaphoreType.DMA((3,)),
+            pltpu.SemaphoreType.DMA((2 * max(1, ff // 512) + 1,)),
             pltpu.SemaphoreType.DMA((2 * n,)),
             pltpu.SemaphoreType.DMA((2 * n,)),
             pltpu.SemaphoreType.DMA((2 * n,)),
@@ -509,69 +523,84 @@
     def place(free, at):
         return tuple(at.get(b, slice(None)) for b in free)
 
+    top = range(bits - 1, -1, -1)
+    width = mine.shape[-1]
+    spot = tuple(bit[b] for b in top)
     copies = []
+
+    def start_sum(f, j):
+        start, size = cols[f]
+        order = orders[f % 2]
+        b = order[j]
+        there = place([x for x in top if x not in order[:j]], {b: 1 - bit[b]})
+        if j == 0:
+            src = mine.at[there + (slice(None), pl.ds(start, size))]
+        else:
+            src = sums[f][j - 1].at[there]
+        copy = pltpu.make_async_remote_copy(
+            src_ref=src,
+            dst_ref=came[f][j],
+            send_sem=rs_send.at[f * bits + j],
+            recv_sem=rs_recv.at[f * bits + j],
+            device_id={"exp": partner[b]},
+            device_id_type=MESH,
+        )
+        copy.start()
+        copies.append(copy)
+        return copy
+
+    def finish_sum(f, j, copy):
+        start, size = cols[f]
+        order = orders[f % 2]
+        b = order[j]
+        here = place([x for x in top if x not in order[:j]], {b: bit[b]})
+        copy.wait_recv()
+        if j == 0:
+            own = mine[here + (slice(None), pl.ds(start, size))]
+        else:
+            own = sums[f][j - 1][here]
+        sums[f][j][...] = (
+            own.astype(jnp.float32) + came[f][j][...].astype(jnp.float32)
+        ).astype(jnp.bfloat16)
+
+    def start_spread(f, j):
+        start, size = cols[f]
+        order = orders[f % 2]
+        if f == len(cols) - 1:
+            size = size + extra.shape[-1]
+        at = place(top, {b: bit[b] for b in order[: j + 1]})
+        block = every.at[at + (slice(None), pl.ds(start, size))]
+        copy = pltpu.make_async_remote_copy(
+            src_ref=block,
+            dst_ref=block,
+            send_sem=ag_send.at[f * bits + j],
+            recv_sem=ag_recv.at[f * bits + j],
+            device_id={"exp": partner[order[j]]},
+            device_id_type=MESH,
+        )
+        copy.start()
+        copies.append(copy)
+        return copy
+
+    if spread:
+        every[spot + (slice(None), pl.ds(width, extra.shape[-1]))] = extra[...]
+    flying = [start_sum(f, 0) for f in range(len(cols))]
     for j in range(bits):
-        stage = []
         for f, (start, size) in enumerate(cols):
-            b = orders[f][j]
-            free = [x for x in range(bits - 1, -1, -1) if x not in orders[f][:j]]
-            there = place(free, {b: 1 - bit[b]})
-            if j == 0:
-                src = mine.at[there + (slice(None), pl.ds(start, size))]
+            finish_sum(f, j, flying[f])
+            if j < bits - 1:
+                flying[f] = start_sum(f, j + 1)
             else:
-                src = sums[f][j - 1].at[there]
-            copy = pltpu.make_async_remote_copy(
-                src_ref=src,
-                dst_ref=came[f][j],
-                send_sem=rs_send.at[f * bits + j],
-                recv_sem=rs_recv.at[f * bits + j],
-                device_id={"exp": partner[b]},
-                device_id_type=MESH,
-            )
-            copy.start()
-            stage.append(copy)
-        for f, (start, size) in enumerate(cols):
-            b = orders[f][j]
-            free = [x for x in range(bits - 1, -1, -1) if x not in orders[f][:j]]
-            here = place(free, {b: bit[b]})
-            stage[f].wait_recv()
-            if j == 0:
-                own = mine[here + (slice(None), pl.ds(start, size))]
-            else:
-                own = sums[f][j - 1][here]
-            sums[f][j][...] = (
-                own.astype(jnp.float32) + came[f][j][...].astype(jnp.float32)
-            ).astype(jnp.bfloat16)
-        copies += stage
-
-    spot = tuple(bit[b] for b in range(bits - 1, -1, -1))
-    for f, (start, size) in enumerate(cols):
-        out[:, pl.ds(start, size)] = sums[f][bits - 1][...]
-        if spread:
-            every[spot + (slice(None), pl.ds(start, size))] = sums[f][bits - 1][...]
+                if spread:
+                    every[spot + (slice(None), pl.ds(start, size))] = sums[f][j][...]
+                    flying[f] = start_spread(f, j)
+                out[:, pl.ds(start, size)] = sums[f][j][...]
     if spread:
-        width = mine.shape[-1]
-        more = extra.shape[-1]
-        every[spot + (slice(None), pl.ds(width, more))] = extra[...]
         for j in reversed(range(bits)):
-            stage = []
-            for f, (start, size) in enumerate(cols):
-                size = size + (more if f == 1 else 0)
-                at = place(range(bits - 1, -1, -1), {b: bit[b] for b in orders[f][: j + 1]})
-                block = every.at[at + (slice(None), pl.ds(start, size))]
-                copy = pltpu.make_async_remote_copy(
-                    src_ref=block,
-                    dst_ref=block,
-                    send_sem=ag_send.at[f * bits + j],
-                    recv_sem=ag_recv.at[f * bits + j],
-                    device_id={"exp": partner[orders[f][j]]},
-                    device_id_type=MESH,
-                )
-                copy.start()
-                stage.append(copy)
-            for copy in stage:
-                copy.wait_recv()
-            copies += stage
+            for f in range(len(cols)):
+                flying[f].wait_recv()
+                if j > 0:
+                    flying[f] = start_spread(f, j - 1)
     for copy in copies:
         copy.wait_send()
 
@@ -582,15 +611,16 @@
     total, width = rows_in.shape
     rows = total // n_exp
     spread = extra is not None
-    first = (width // 2 + 127) // 128 * 128
-    cols = ((0, first), (first, width - first))
+    lanes = width // 128
+    sizes = [128 * ((lanes + 3 - f) // 4) for f in range(4)]
+    cols = tuple((sum(sizes[:f]), sizes[f]) for f in range(4))
     vmem = pl.BlockSpec(memory_space=pltpu.VMEM)
     shapes = []
     for _ in range(2):
         for _, size in cols:
             for j in range(bits):
                 shapes.append(pltpu.VMEM((2,) * (bits - 1 - j) + (rows, size), jnp.bfloat16))
-    shapes += [pltpu.SemaphoreType.DMA((2 * bits,))] * (4 if spread else 2)
+    shapes += [pltpu.SemaphoreType.DMA((4 * bits,))] * (4 if spread else 2)
     out_shape = [jax.ShapeDtypeStruct((rows, width), jnp.bfloat16)]
     operands = [rows_in.reshape((2,) * bits + (rows, width))]
     if spread:

time: 336 us -> 310 us (0.923)
  Pallas kernels: 317 us -> 291 us
    pallas_call x1, Pallas kernels: 148 us -> 134 us  [expert_layer(): pl.pallas_call(partial(expert_kernel, n_ctx), out_shape=jax.ShapeDtypeStr...]
    pallas_call x2, Pallas kernels: 70.9 us -> 59.1 us  [exp_sum(): pl.pallas_call(partial(exp_kernel, bits, cols, spread), out_shape=out_sha...]
where the time goes in v3:
time: 310 us; the launch traced here: 309 us
  Pallas kernels  291 us (94%)
  matrix products  9.98 us (3%)
  local copies, waits for them, and re-layouts  4.58 us (1%)
  other arithmetic  3.64 us (1%)
    pallas_call x1, Pallas kernels, expert_layer(): pl.pallas_call(partial(expert_kernel, n_ctx), out_shape=jax.ShapeDtypeStr...  134 us
    pallas_call x1, Pallas kernels, attend(): pl.pallas_call(partial(attend_kernel, n_ctx, score_scale), out_shape=jax....  97.8 us
    pallas_call x2, Pallas kernels, exp_sum(): pl.pallas_call(partial(exp_kernel, bits, cols, spread), out_shape=out_sha...  59.1 us

profile of v3, /device:TPU:0, one launch (start us, length us, event | category | flops | bytes accessed | tf_op | source)
XLA Modules:
  0.0 309.5 jit_solution(1355231062109612362)
XLA Ops:
  0.7 0.7 convert_element_type.28
  1.3 0.7 pad_maximum_fusion.1
  2.0 0.1 copy.20
  2.2 0.9 copy.18
  3.0 1.8 pad_maximum_fusion.kv
  4.8 97.8 %attend.1 = bf16[1024,1792]{1,0:T(8,128)(2,1)} custom-call(bf16[256,2048]{1,0:T(8,128)(2,1)} %q_nope.1, bf16[256,1024]{1,0:T(8,128)(2,1)} %q_rope.1, bf16[256,640]{1,0:T(8,128)(2,1)} %pad_maximum_fusion.kv, bf16[16,128,512]{2,1,0:T(8,128)(2,1)} %w_uk.1, bf16[16,512,128]{2,1,0:T(8,128)(2,1)} %w_uv.1, bf16[2048,1792]{1,0:T(8,128)(2,1)} %wo_hbm.1), custom_call_target="tpu_custom_call" | custom-call | flops 7516192768 | bytes 7340032 | tf_op jit(solution)/shard_map/attend/pallas_call | solution.py:469
  102.6 0.0 copy-start
  102.6 2.0 copy-done
  104.6 39.5 %exp_sum_spread.1 = (bf16[128,1792]{1,0:T(8,128)(2,1)S(1)}, bf16[2,2,2,128,1920]{4,3,2,1,0:T(8,128)(2,1)S(1)}) custom-call(bf16[2,2,2,128,1792]{4,3,2,1,0:T(8,128)(2,1)S(1)} %bitcast.14, bf16[128,128]{1,0:T(8,128)(2,1)S(1)} %pad.4.refs_1_), custom_call_target="tpu_custom_call" | custom-call | flops 3670016 | bytes 7340032 | tf_op jit(solution)/shard_map/exp_sum_spread/pallas_call | solution.py:630
  144.2 0.2 fusion.17
  144.4 0.3 select_reduce_fusion
  144.7 0.2 fusion.11
  144.9 4.4 %fusion.2.x = bf16[768,1792]{1,0:T(8,128)(2,1)} fusion(bf16[1024,1920]{1,0:T(8,128)(2,1)S(1)} %bitcast.18, s32[1024]{0:T(1024)S(1)} %fusion.11), kind=kOutput, calls=%fused_computation.3 | convolution fusion | flops 2820734976 | bytes 6426624 | tf_op jit(solution)/shard_map/dot_general | solution.py:693
  149.3 133.7 %expert_layer.1 = bf16[768,1792]{1,0:T(8,128)(2,1)} custom-call(bf16[768,1792]{1,0:T(8,128)(2,1)} %fusion.2.x, bf16[1792,2048]{1,0:T(8,128)(2,1)} %bitcast.19, bf16[1792,2048]{1,0:T(8,128)(2,1)} %bitcast.20, bf16[2048,1792]{1,0:T(8,128)(2,1)} %bitcast.21), custom_call_target="tpu_custom_call" | custom-call | flops 16911433728 | bytes 22020096 | tf_op jit(solution)/shard_map/expert_layer/pallas_call | solution.py:208
  283.0 5.4 %convolution_convert_fusion = bf16[1024,1792]{1,0:T(8,128)(2,1)S(1)} fusion(bf16[768,1792]{1,0:T(8,128)(2,1)} %expert_layer.1, bf16[1024]{0:T(1024)(128)(2,1)S(1)} %select_reduce_fusion, s32[1024]{0:T(1024)S(1)} %fusion.11), kind=kOutput, calls=%fused_computation | convolution fusion | flops 2821980160 | bytes 6428672 | tf_op jit(solution)/shard_map/dot_general | solution.py:698
  288.4 19.6 %exp_sum.1 = bf16[128,1792]{1,0:T(8,128)(2,1)S(1)} custom-call(bf16[2,2,2,128,1792]{4,3,2,1,0:T(8,128)(2,1)S(1)} %bitcast.15), custom_call_target="tpu_custom_call" | custom-call | flops 3670016 | bytes 7340032 | tf_op jit(solution)/shard_map/exp_sum/pallas_call | solution.py:630
  308.0 0.8 copy.23
  308.7 0.8 copy.24
  (3 shorter events, 0.0 us)
Async XLA Ops:
  102.6 2.0 copy-start

commit v4 on v3

--- a/solution.py
+++ b/solution.py
@@ -13,21 +13,21 @@
 CHUNK = 16
 SLACK = 2
 AHEAD = 3
-BLOCK = 128
 
 
 def expert_kernel(
-    n_ctx, x, wg_hbm, wu_hbm, wd_hbm, out, wg, wu, wd, part, held, hid,
+    n_ctx, cap, slots, gates, x, wg_hbm, wu_hbm, wd_hbm, out, wg, wu, wd, picked, part, held, hid,
     w_sem, rs_send, rs_recv, ag_send, ag_recv,
 ):
     p = lax.axis_index("ctx")
     last = n_ctx - 1
-    rows = x.shape[0]
+    sources, toks = slots.shape
+    rows = sources * cap
     half = rows // 2
-    ff = wg.shape[1]
+    width, ff = wg.shape
     n = half // CHUNK
-    per = BLOCK // CHUNK
-    blocks = half // BLOCK
+    per = cap // CHUNK
+    blocks = sources // 2
     tile = 512 if ff % 512 == 0 else ff
 
     tiles = ff // tile
@@ -81,36 +81,57 @@
             device_id_type=MESH,
         )
 
+    def placing(b):
+        slot = lax.broadcasted_iota(jnp.int32, (cap, toks), 0)
+        return jnp.where(slots[pl.ds(b, 1), :] == slot, 1.0, 0.0).astype(jnp.bfloat16)
+
+    def pick(d, block):
+        b = d * blocks + block
+        tokens = x[pl.ds(pl.multiple_of(b * toks, toks), toks), pl.ds(0, width)]
+        picked[...] = jnp.dot(
+            placing(b), tokens, preferred_element_type=jnp.float32
+        ).astype(picked.dtype)
+
     def gate_up_tile(d, block, c):
-        at = pl.ds(pl.multiple_of(d * half + block * BLOCK, BLOCK), BLOCK)
+        at = pl.ds(pl.multiple_of(d * half + block * cap, CHUNK), cap)
         base = pl.multiple_of(c * tile, tile)
         above = pl.multiple_of(ff + c * tile, tile)
         part[at, pl.ds(base, tile)] = jnp.dot(
-            x[at, :], wg[:, pl.ds(base, tile)], preferred_element_type=jnp.float32
+            picked[...], wg[:, pl.ds(base, tile)], preferred_element_type=jnp.float32
         ).astype(part.dtype)
         part[at, pl.ds(above, tile)] = jnp.dot(
-            x[at, :], wu[:, pl.ds(base, tile)], preferred_element_type=jnp.float32
+            picked[...], wu[:, pl.ds(base, tile)], preferred_element_type=jnp.float32
         ).astype(part.dtype)
 
     def gate_up(d, block):
+        pick(d, block)
+
         @pl.loop(0, tiles)
         def _(c):
             gate_up_tile(d, block, c)
 
-    width = out.shape[1]
     down_tile = 256 if width % 256 == 0 else 128
 
     def down(d, block):
-        at = pl.ds(pl.multiple_of(d * half + block * BLOCK, BLOCK), BLOCK)
+        b = d * blocks + block
+        at = pl.ds(pl.multiple_of(d * half + block * cap, CHUNK), cap)
+        to = pl.ds(pl.multiple_of(b * toks, toks), toks)
+        place = placing(b)
+        gate = gates[to, :]
 
         @pl.loop(0, width // down_tile)
         def _(c):
             cols = pl.ds(pl.multiple_of(c * down_tile, down_tile), down_tile)
-            out[at, cols] = jnp.dot(
+            expert_out = jnp.dot(
                 hid[at, :], wd[:, cols], preferred_element_type=jnp.float32
-            ).astype(out.dtype)
+            ).astype(jnp.bfloat16)
+            own = lax.dot_general(
+                place, expert_out, (((0,), (0,)), ((), ())), preferred_element_type=jnp.float32
+            )
+            out[to, cols] = (own * gate).astype(out.dtype)
 
     first = (2 * p > last).astype(jnp.int32)
+    pick(first, 0)
     for c in range(tiles):
         loads[2 * c].wait()
         loads[2 * c + 1].wait()
@@ -200,21 +221,22 @@
                 ag_copy(d, t).wait_send()
 
 
-def expert_layer(rows_in, gate_w, up_w, down_w):
+def expert_layer(slots, gates, tokens, gate_w, up_w, down_w, cap):
     n_ctx = lax.axis_size("ctx")
-    rows, width = rows_in.shape
-    ff = gate_w.shape[1]
+    width, ff = gate_w.shape
+    rows = slots.shape[0] * cap
     n = rows // 2 // CHUNK
     return pl.pallas_call(
-        partial(expert_kernel, n_ctx),
-        out_shape=jax.ShapeDtypeStruct((rows, width), jnp.bfloat16),
-        in_specs=[pl.BlockSpec(memory_space=pltpu.VMEM)]
+        partial(expert_kernel, n_ctx, cap),
+        out_shape=jax.ShapeDtypeStruct((slots.size, width), jnp.bfloat16),
+        in_specs=[pl.BlockSpec(memory_space=pltpu.VMEM)] * 3
         + [pl.BlockSpec(memory_space=pl.ANY)] * 3,
         out_specs=pl.BlockSpec(memory_space=pltpu.VMEM),
         scratch_shapes=[
             pltpu.VMEM((width, ff), jnp.bfloat16),
             pltpu.VMEM((width, ff), jnp.bfloat16),
             pltpu.VMEM((ff, width), jnp.bfloat16),
+            pltpu.VMEM((cap, width), jnp.bfloat16),
             pltpu.VMEM((rows, 2 * ff), jnp.bfloat16),
             pltpu.VMEM((rows, 2 * ff), jnp.bfloat16),
             pltpu.VMEM((rows, ff), jnp.bfloat16),
@@ -231,7 +253,8 @@
             flops=6 * rows * width * ff, bytes_accessed=6 * width * ff, transcendentals=rows * ff
         ),
         name="expert_layer",
-    )(rows_in, gate_w, up_w, down_w)
+    )(slots, gates, tokens, gate_w, up_w, down_w)
+
 
 def attend_kernel(
     n_ctx, score_scale, q_nope, q_rope, kv, w_uk, w_uv, wo_hbm, out, keys, queries, heads, acc, wo,
@@ -673,7 +696,6 @@
     attn_out, gathered = exp_sum(partial_out, routing, 2)
     total, width = partial_out.shape
     capacity = 3 * out_rows * top_count // (2 * n_exp)
-    slot_total = n_exp * capacity
     ids = gathered[:, width : width + top_count].astype(jnp.float32)
     gates = gathered[:, width + top_count : width + 2 * top_count].astype(jnp.float32)
     named = ids == lax.axis_index("exp").astype(jnp.float32)
@@ -686,18 +708,8 @@
         (((1,), (1,)), ((), ())),
         preferred_element_type=jnp.float32,
     ).astype(jnp.int32)
-    slots = ranks + capacity * jnp.arange(n_exp, dtype=jnp.int32)[:, None]
-    slots = jnp.where(chosen, slots.reshape(total), -1)
-    slot_range = jnp.arange(slot_total, dtype=jnp.int32)
-    placing = (slots[None, :] == slot_range[:, None]).astype(jnp.bfloat16)
-    arrived = jnp.dot(
-        placing, gathered[:, :width], preferred_element_type=jnp.float32
-    ).astype(jnp.bfloat16)
-    expert_out = expert_layer(arrived, w_gate[0], w_up[0], w_down[0])
-    weighting = jnp.where(slots[:, None] == slot_range[None, :], gate[:, None], 0.0)
-    share = jnp.dot(
-        weighting.astype(jnp.bfloat16), expert_out, preferred_element_type=jnp.float32
-    ).astype(jnp.bfloat16)
+    slots = jnp.where(chosen.reshape(n_exp, out_rows), ranks, -1)
+    share = expert_layer(slots, gate[:, None], gathered, w_gate[0], w_up[0], w_down[0], capacity)
     return (attn_out, exp_sum(share, None, 3))
 
 

time: 310 us -> 311 us (level)
  matrix products: 9.98 us -> 1.17 us
  Pallas kernels: 291 us -> 297 us
  local copies, waits for them, and re-layouts: 4.58 us -> 8.12 us
    dot_general x2 -> x0, matrix products: 9.77 us -> none  [the longest x1 5.37 us: local(): jnp.dot(weighting.astype(jnp.bfloat16), expert_out, preferred_element_typ...]
    pallas_call x1, Pallas kernels: 134 us -> 140 us  [expert_layer(): pl.pallas_call(partial(expert_kernel, n_ctx, cap), out_shape=jax.ShapeDty...]
    unnamed x5 -> x9, local copies, waits for them, and re-layouts: 4.44 us -> 6.95 us
where the time goes in v4:
time: 311 us; the launch traced here: 310 us
  Pallas kernels  297 us (95%)
  local copies, waits for them, and re-layouts  8.12 us (3%)
  other arithmetic  3.63 us (1%)
    pallas_call x1, Pallas kernels, expert_layer(): pl.pallas_call(partial(expert_kernel, n_ctx, cap), out_shape=jax.ShapeDty...  140 us
    pallas_call x1, Pallas kernels, attend(): pl.pallas_call(partial(attend_kernel, n_ctx, score_scale), out_shape=jax....  97.8 us
    pallas_call x2, Pallas kernels, exp_sum(): pl.pallas_call(partial(exp_kernel, bits, cols, spread), out_shape=out_sha...  59 us
    unnamed x9, local copies, waits for them, and re-layouts  6.95 us

profile of v4, /device:TPU:0, one launch (start us, length us, event | category | flops | bytes accessed | tf_op | source)
XLA Modules:
  0.0 310.3 jit_solution(16412350856420322207)
XLA Ops:
  0.6 0.7 convert_element_type.18
  1.3 0.7 pad_maximum_fusion.1
  2.0 0.1 copy.25
  2.2 0.9 copy.23
  3.0 1.8 pad_maximum_fusion.kv
  4.8 97.8 %attend.1 = bf16[1024,1792]{1,0:T(8,128)(2,1)} custom-call(bf16[256,2048]{1,0:T(8,128)(2,1)} %q_nope.1, bf16[256,1024]{1,0:T(8,128)(2,1)} %q_rope.1, bf16[256,640]{1,0:T(8,128)(2,1)} %pad_maximum_fusion.kv, bf16[16,128,512]{2,1,0:T(8,128)(2,1)} %w_uk.1, bf16[16,512,128]{2,1,0:T(8,128)(2,1)} %w_uv.1, bf16[2048,1792]{1,0:T(8,128)(2,1)} %wo_hbm.1), custom_call_target="tpu_custom_call" | custom-call | flops 7516192768 | bytes 7340032 | tf_op jit(solution)/shard_map/attend/pallas_call | solution.py:492
  102.6 0.0 copy-start
  102.6 2.0 copy-done
  104.6 39.5 %exp_sum_spread.1 = (bf16[128,1792]{1,0:T(8,128)(2,1)S(1)}, bf16[2,2,2,128,1920]{4,3,2,1,0:T(8,128)(2,1)S(1)}) custom-call(bf16[2,2,2,128,1792]{4,3,2,1,0:T(8,128)(2,1)S(1)} %bitcast.10, bf16[128,128]{1,0:T(8,128)(2,1)S(1)} %pad.4.refs_1_), custom_call_target="tpu_custom_call" | custom-call | flops 3670016 | bytes 7340032 | tf_op jit(solution)/shard_map/exp_sum_spread/pallas_call | solution.py:653
  144.2 0.0 copy-start.2
  144.2 0.2 fusion.6
  144.4 1.2 fusion.slots
  145.6 0.5 copy-done.2
  146.0 0.3 select_reduce_fusion
  146.3 1.0 copy.26.gates
  147.3 139.8 %expert_layer.1 = bf16[1024,1792]{1,0:T(8,128)(2,1)} custom-call(s32[8,128]{1,0:T(8,128)} %fusion.slots, f32[1024,1]{1,0:T(8,128)} %copy.26.gates, bf16[1024,1920]{1,0:T(8,128)(2,1)} %bitcast.14, bf16[1792,2048]{1,0:T(8,128)(2,1)} %bitcast.16, bf16[1792,2048]{1,0:T(8,128)(2,1)} %bitcast.17, bf16[2048,1792]{1,0:T(8,128)(2,1)} %bitcast.18), custom_call_target="tpu_custom_call" | custom-call | flops 16911433728 | bytes 22020096 | tf_op jit(solution)/shard_map/expert_layer/pallas_call | solution.py:229
  287.2 0.0 copy-start.1
  287.2 2.0 copy-done.1
  289.2 19.5 %exp_sum.1 = bf16[128,1792]{1,0:T(8,128)(2,1)S(1)} custom-call(bf16[2,2,2,128,1792]{4,3,2,1,0:T(8,128)(2,1)S(1)} %bitcast.11), custom_call_target="tpu_custom_call" | custom-call | flops 3670016 | bytes 7340032 | tf_op jit(solution)/shard_map/exp_sum/pallas_call | solution.py:653
  308.8 0.8 copy.29
  309.5 0.8 copy.30
  (2 shorter events, 0.0 us)
Async XLA Ops:
  102.6 2.0 copy-start
  144.2 1.9 copy-start.2
  287.2 2.0 copy-start.1
